TPU v7x, 32 devices: a whole 2x2x4 slice. The times are simulated.
32 devices in a mesh: section: 4 (over x, core), dp: 8 (over z, y).
Axes of the slice: x: 2, y: 2, z: 4, core: 2. Of those that a mesh axis runs over, the one named last changes fastest.
Arguments:
- inputs: bfloat16 [2, 4096, 768], P(None, 'dp'), may hold values from -6 to 6
- segment_ids: int32 [2, 4096], P(None, 'dp'), may hold values from 0 to 31, never falling along the last dimension, each value on 1 to 512 neighbouring positions
- w_in: bfloat16 [4, 768, 3072], P('section'), may hold values from -3 to 3
- w_down: bfloat16 [4, 3072, 768], P('section'), may hold values from -0.109375 to 0.109375
- vec_in: float32 [4, 3072], P('section'), may hold values from -3 to 3
- vec_out: float32 [4, 2304], P('section'), may hold values from -2 to 2
- cotangent: bfloat16 [2, 4096, 768], P(None, 'dp'), may hold values from -6 to 6
Outputs:
- mixed: bfloat16 [2, 4096, 768], P(None, 'dp', 'section')
- input_grad: bfloat16 [2, 4096, 768], P(None, 'dp', 'section')
- grad_w_in: float32 [4, 768, 3072], P('section', 'dp')
- grad_w_down: float32 [4, 3072, 768], P('section', 'dp')
- grad_vec_in: float32 [4, 3072], P('section', 'dp')
- grad_vec_out: float32 [4, 2304], P('section', 'dp')
Inputs may be any that keep to these rules, and one draw needn't show every extreme that they name: Along a row of segment_ids the ids never fall; one id covers at most 512 rows, and some id covers exactly 512.
All inputs are finite; a program needn't handle non-finite values.
Results may differ from a plain program's by a relative error of at most 0.024.
Values may be sent and summed in bfloat16 or wider, within the bound.
A program may use at most 384 MiB of HBM per device.

v0:
```python
import math

import jax
import jax.numpy as jnp
from jax import lax
from jax.sharding import PartitionSpec as P

HEADS = 12
BLK = 512


EPS = 1e-06
NEG = -1e30
CONTRACT_ROWS = (((0,), (0,)), ((), ()))
CONTRACT_COLS = (((1,), (1,)), ((), ()))


def passed_along(block, axis, distance):
    devices = range(lax.axis_size(axis))
    route = [(i - distance, i) for i in devices if i - distance in devices]
    return lax.ppermute(block, axis, route)


def layer_norm(summed, norm_gain, norm_bias):
    average = jnp.mean(summed, axis=-1, keepdims=True)
    centred = summed - average
    spread = jnp.mean(centred * centred, axis=-1, keepdims=True)
    return centred * lax.rsqrt(spread + EPS) * norm_gain + norm_bias


def rotary_tables(seg_rows, head_dim):
    blocks = seg_rows.reshape(-1, BLK)
    offsets = jnp.arange(BLK, dtype=jnp.int32)
    same_doc = blocks[:, :, None] == blocks[:, None, :]
    opener = jnp.min(jnp.where(same_doc, offsets[None, None, :], BLK), axis=2)
    places = (offsets[None, :] - opener).astype(jnp.float32).reshape(-1)
    frequency = jnp.exp(
        jnp.arange(head_dim // 2, dtype=jnp.float32) * (-2.0 * math.log(10000.0) / head_dim)
    )
    angles = places[:, None] * frequency[None, :]
    return (jnp.cos(angles)[:, None, :], jnp.sin(angles)[:, None, :])


def rotate(values, cos_tab, sin_tab):
    half_dim = values.shape[-1] // 2
    front_half = values[..., :half_dim]
    back_half = values[..., half_dim:]
    return jnp.concatenate(
        [front_half * cos_tab - back_half * sin_tab, back_half * cos_tab + front_half * sin_tab],
        axis=-1,
    )


def attention_forward(section_in, seg_rows, w_main, bias_in, bias_out):
    row_count, model_width = section_in.shape
    head_dim = model_width // HEADS
    score_scale = head_dim ** (-0.5)
    cos_tab, sin_tab = rotary_tables(seg_rows, head_dim)
    project = (
        jnp.dot(section_in, w_main[:, : 3 * model_width], preferred_element_type=jnp.float32)
        + bias_in[: 3 * model_width]
    )
    heads_shape = (row_count, HEADS, head_dim)
    queries = rotate(project[:, :model_width].reshape(heads_shape), cos_tab, sin_tab).astype(
        jnp.bfloat16
    )
    keys_rot = rotate(
        project[:, model_width : 2 * model_width].reshape(heads_shape), cos_tab, sin_tab
    ).astype(jnp.bfloat16)
    values = project[:, 2 * model_width :].astype(jnp.bfloat16).reshape(heads_shape)

    def attend(pieces):
        q_blk, k_blk, v_blk, seg_blk = pieces
        scores = (
            jnp.einsum("qhd,khd->hqk", q_blk, k_blk, preferred_element_type=jnp.float32)
            * score_scale
        )
        same_doc = (seg_blk[:, None] == seg_blk[None, :])[None]
        scores = jnp.where(same_doc, scores, NEG)
        row_peak = jnp.max(scores, axis=-1, keepdims=True)
        exp_scores = jnp.exp(scores - row_peak)
        row_total = jnp.sum(exp_scores, axis=-1, keepdims=True)
        probs_low = (exp_scores / row_total).astype(jnp.bfloat16)
        attended = jnp.einsum("hqk,khd->qhd", probs_low, v_blk, preferred_element_type=jnp.float32)
        return (attended.reshape(BLK, model_width), (row_peak + jnp.log(row_total))[:, :, 0])

    block_shape = (-1, BLK, HEADS, head_dim)
    attended, log_total = lax.map(
        attend,
        (
            queries.reshape(block_shape),
            keys_rot.reshape(block_shape),
            values.reshape(block_shape),
            seg_rows.reshape(-1, BLK),
        ),
    )
    attended_low = attended.reshape(row_count, model_width).astype(jnp.bfloat16)
    branch = (
        jnp.dot(attended_low, w_main[:, 3 * model_width :], preferred_element_type=jnp.float32)
        + bias_out[2 * model_width :]
    )
    summed = branch + section_in.astype(jnp.float32)
    output = layer_norm(summed, bias_out[:model_width], bias_out[model_width : 2 * model_width])
    kept_low = jnp.concatenate(
        [
            queries.reshape(row_count, model_width),
            keys_rot.reshape(row_count, model_width),
            values.reshape(row_count, model_width),
            attended_low,
        ],
        axis=1,
    )
    kept_wide = jnp.zeros((row_count, 4 * model_width), jnp.float32)
    return (output, (kept_wide, kept_low, summed, log_total))


def feed_forward(section_in, w_main, w_low, bias_in, bias_out):
    row_count, model_width = section_in.shape
    hidden = jnp.dot(section_in, w_main, preferred_element_type=jnp.float32) + bias_in
    active = jax.nn.gelu(hidden, approximate=True).astype(jnp.bfloat16)
    branch = (
        jnp.dot(active, w_low, preferred_element_type=jnp.float32) + bias_out[2 * model_width :]
    )
    summed = branch + section_in.astype(jnp.float32)
    output = layer_norm(summed, bias_out[:model_width], bias_out[model_width : 2 * model_width])
    log_total = jnp.zeros((row_count // BLK, HEADS, BLK), jnp.float32)
    return (output, (hidden, active, summed, log_total))


def attention_backward(seg_rows, incoming, kept_state, w_main, bias_out):
    _, kept_low, summed, log_total = kept_state
    row_count = summed.shape[0]
    model_width = summed.shape[1]
    head_dim = model_width // HEADS
    score_scale = head_dim ** (-0.5)
    cos_tab, sin_tab = rotary_tables(seg_rows, head_dim)
    _, pull_back = jax.vjp(
        layer_norm, summed, bias_out[:model_width], bias_out[model_width : 2 * model_width]
    )
    grad_sum, grad_gain, grad_shift = pull_back(incoming.astype(jnp.float32))
    grad_branch = grad_sum.astype(jnp.bfloat16)
    grad_out_bias = jnp.sum(grad_branch, axis=0, dtype=jnp.float32)
    queries = kept_low[:, :model_width]
    keys_rot = kept_low[:, model_width : 2 * model_width]
    values = kept_low[:, 2 * model_width : 3 * model_width]
    w_out = w_main[:, 3 * model_width :]
    grad_attended = lax.dot_general(
        grad_branch, w_out, CONTRACT_COLS, preferred_element_type=jnp.float32
    ).astype(jnp.bfloat16)

    def attend_back(pieces):
        q_blk, k_blk, v_blk, g_blk, seg_blk, lse_blk = pieces
        scores = (
            jnp.einsum("qhd,khd->hqk", q_blk, k_blk, preferred_element_type=jnp.float32)
            * score_scale
        )
        same_doc = (seg_blk[:, None] == seg_blk[None, :])[None]
        probs_full = jnp.where(same_doc, jnp.exp(scores - lse_blk[:, :, None]), 0.0)
        probs_low = probs_full.astype(jnp.bfloat16)
        grad_probs = jnp.einsum("qhd,khd->hqk", g_blk, v_blk, preferred_element_type=jnp.float32)
        row_inner = jnp.sum(probs_full * grad_probs, axis=-1, keepdims=True)
        grad_scores = (probs_full * (grad_probs - row_inner)).astype(jnp.bfloat16)
        grad_q = (
            jnp.einsum("hqk,khd->qhd", grad_scores, k_blk, preferred_element_type=jnp.float32)
            * score_scale
        )
        grad_k = (
            jnp.einsum("hqk,qhd->khd", grad_scores, q_blk, preferred_element_type=jnp.float32)
            * score_scale
        )
        grad_v = jnp.einsum("hqk,qhd->khd", probs_low, g_blk, preferred_element_type=jnp.float32)
        return (grad_q, grad_k, grad_v)

    block_shape = (-1, BLK, HEADS, head_dim)
    heads_shape = (row_count, HEADS, head_dim)
    grad_q, grad_k, grad_v = lax.map(
        attend_back,
        (
            queries.reshape(block_shape),
            keys_rot.reshape(block_shape),
            values.reshape(block_shape),
            grad_attended.reshape(block_shape),
            seg_rows.reshape(-1, BLK),
            log_total,
        ),
    )
    grad_proj = jnp.concatenate(
        [
            rotate(grad_q.reshape(heads_shape), cos_tab, -sin_tab).reshape(row_count, model_width),
            rotate(grad_k.reshape(heads_shape), cos_tab, -sin_tab).reshape(row_count, model_width),
            grad_v.reshape(row_count, model_width),
        ],
        axis=1,
    ).astype(jnp.bfloat16)
    grad_input = (
        lax.dot_general(
            grad_proj,
            w_main[:, : 3 * model_width],
            CONTRACT_COLS,
            preferred_element_type=jnp.float32,
        )
        + grad_sum
    )
    grad_wide = jnp.concatenate(
        [grad_proj, jnp.zeros((row_count, model_width), jnp.bfloat16)], axis=1
    )
    return (
        grad_input,
        (grad_wide, grad_branch, jnp.concatenate([grad_gain, grad_shift, grad_out_bias])),
    )


def feed_backward(incoming, kept_state, w_main, w_low, bias_out):
    hidden, _, summed, _ = kept_state
    model_width = summed.shape[1]
    _, pull_back = jax.vjp(
        layer_norm, summed, bias_out[:model_width], bias_out[model_width : 2 * model_width]
    )
    grad_sum, grad_gain, grad_shift = pull_back(incoming.astype(jnp.float32))
    grad_branch = grad_sum.astype(jnp.bfloat16)
    grad_out_bias = jnp.sum(grad_branch, axis=0, dtype=jnp.float32)
    grad_active = lax.dot_general(
        grad_branch, w_low, CONTRACT_COLS, preferred_element_type=jnp.float32
    )
    _, gelu_pull = jax.vjp(lambda inner_value: jax.nn.gelu(inner_value, approximate=True), hidden)
    grad_hidden = gelu_pull(grad_active)[0].astype(jnp.bfloat16)
    grad_input = (
        lax.dot_general(grad_hidden, w_main, CONTRACT_COLS, preferred_element_type=jnp.float32)
        + grad_sum
    )
    return (
        grad_input,
        (grad_hidden, grad_branch, jnp.concatenate([grad_gain, grad_shift, grad_out_bias])),
    )


def attention_weights(left_in, left_mid, grad_wide, grad_narrow):
    model_width = left_in.shape[1]
    grad_qkv = lax.dot_general(
        left_in, grad_wide[:, : 3 * model_width], CONTRACT_ROWS, preferred_element_type=jnp.float32
    )
    grad_out = lax.dot_general(
        left_mid[:, 3 * model_width :],
        grad_narrow,
        CONTRACT_ROWS,
        preferred_element_type=jnp.float32,
    )
    return (
        jnp.concatenate([grad_qkv, grad_out], axis=1),
        jnp.zeros((left_mid.shape[1], model_width), jnp.float32),
    )


def feed_weights(left_in, left_mid, grad_wide, grad_narrow):
    grad_main = lax.dot_general(
        left_in, grad_wide, CONTRACT_ROWS, preferred_element_type=jnp.float32
    )
    grad_low = lax.dot_general(
        left_mid, grad_narrow, CONTRACT_ROWS, preferred_element_type=jnp.float32
    )
    return (grad_main, grad_low)


def on_device(inputs, segment_ids, w_in, w_down, vec_in, vec_out, cotangent):
    section_count = lax.axis_size("section")
    section_id = lax.axis_index("section")
    micro_count, row_count, model_width = inputs.shape
    hidden_width = w_in.shape[2]
    block_count = row_count // BLK
    w_main = w_in[0]
    w_low = w_down[0]
    bias_in = vec_in[0]
    bias_out = vec_out[0]
    even_section = section_id % 2 == 0
    tick_count = micro_count + section_count - 1

    def attention_fwd(section_in, seg_rows):
        return attention_forward(section_in, seg_rows, w_main, bias_in, bias_out)

    def feed_fwd(section_in, seg_rows):
        return feed_forward(section_in, w_main, w_low, bias_in, bias_out)

    def run_forward(section_in, seg_rows):
        return lax.cond(even_section, attention_fwd, feed_fwd, section_in, seg_rows)

    def spare_forward(section_in, seg_rows):
        return (
            jnp.zeros((row_count, model_width), jnp.float32),
            (
                jnp.zeros((row_count, hidden_width), jnp.float32),
                jnp.zeros((row_count, hidden_width), jnp.bfloat16),
                jnp.zeros((row_count, model_width), jnp.float32),
                jnp.zeros((block_count, HEADS, BLK), jnp.float32),
            ),
        )

    def attention_bwd(seg_rows, incoming, kept_state):
        return attention_backward(seg_rows, incoming, kept_state, w_main, bias_out)

    def feed_bwd(seg_rows, incoming, kept_state):
        return feed_backward(incoming, kept_state, w_main, w_low, bias_out)

    def run_backward(seg_rows, incoming, kept_state):
        return lax.cond(even_section, attention_bwd, feed_bwd, seg_rows, incoming, kept_state)

    def spare_backward(seg_rows, incoming, kept_state):
        return (
            jnp.zeros((row_count, model_width), jnp.float32),
            (
                jnp.zeros((row_count, hidden_width), jnp.bfloat16),
                jnp.zeros((row_count, model_width), jnp.bfloat16),
                jnp.zeros((3 * model_width,), jnp.float32),
            ),
        )

    kept_in = jnp.zeros((micro_count + 1, row_count, model_width), jnp.bfloat16)
    kept_wide = jnp.zeros((micro_count + 1, row_count, hidden_width), jnp.float32)
    kept_low = jnp.zeros((micro_count + 1, row_count, hidden_width), jnp.bfloat16)
    kept_sum = jnp.zeros((micro_count + 1, row_count, model_width), jnp.float32)
    kept_lse = jnp.zeros((micro_count + 1, block_count, HEADS, BLK), jnp.float32)
    finals = jnp.zeros((micro_count + 1, row_count, model_width), jnp.bfloat16)
    arrived = jnp.zeros((row_count, model_width), jnp.bfloat16)
    for tick_id in range(tick_count):
        micro_id = tick_id - section_id
        active_tick = (micro_id >= 0) & (micro_id < micro_count)
        store_slot = jnp.where(active_tick, micro_id, micro_count)
        read_slot = jnp.clip(micro_id, 0, micro_count - 1)
        section_in = jnp.where(section_id == 0, inputs[read_slot], arrived)
        seg_rows = segment_ids[read_slot]
        output, kept_state = lax.cond(active_tick, run_forward, spare_forward, section_in, seg_rows)
        kept_in = kept_in.at[store_slot].set(section_in)
        kept_wide = kept_wide.at[store_slot].set(kept_state[0])
        kept_low = kept_low.at[store_slot].set(kept_state[1])
        kept_sum = kept_sum.at[store_slot].set(kept_state[2])
        kept_lse = kept_lse.at[store_slot].set(kept_state[3])
        output_low = output.astype(jnp.bfloat16)
        finals = finals.at[store_slot].set(output_low)
        if tick_id < tick_count - 1:
            arrived = passed_along(output_low, "section", 1)
    returned = jnp.zeros((row_count, model_width), jnp.bfloat16)
    input_grads = jnp.zeros((micro_count + 1, row_count, model_width), jnp.bfloat16)
    grad_wide_buf = jnp.zeros((micro_count + 1, row_count, hidden_width), jnp.bfloat16)
    grad_narrow_buf = jnp.zeros((micro_count + 1, row_count, model_width), jnp.bfloat16)
    vector_terms = jnp.zeros((3 * model_width,), jnp.float32)
    for tick_id in range(tick_count):
        micro_id = tick_id - (section_count - 1 - section_id)
        active_tick = (micro_id >= 0) & (micro_id < micro_count)
        store_slot = jnp.where(active_tick, micro_id, micro_count)
        read_slot = jnp.clip(micro_id, 0, micro_count - 1)
        incoming = jnp.where(section_id == section_count - 1, cotangent[read_slot], returned)
        kept_state = (
            kept_wide[read_slot],
            kept_low[read_slot],
            kept_sum[read_slot],
            kept_lse[read_slot],
        )
        grad_input, (grad_wide, grad_narrow, vector_new) = lax.cond(
            active_tick, run_backward, spare_backward, segment_ids[read_slot], incoming, kept_state
        )
        grad_low = grad_input.astype(jnp.bfloat16)
        input_grads = input_grads.at[store_slot].set(grad_low)
        grad_wide_buf = grad_wide_buf.at[store_slot].set(grad_wide)
        grad_narrow_buf = grad_narrow_buf.at[store_slot].set(grad_narrow)
        vector_terms = vector_terms + vector_new
        if tick_id < tick_count - 1:
            returned = passed_along(grad_low, "section", -1)
    left_in = kept_in[0:micro_count].reshape(-1, model_width)
    left_mid = kept_low[0:micro_count].reshape(-1, hidden_width)
    wide_rows = grad_wide_buf[0:micro_count].reshape(-1, hidden_width)
    narrow_rows = grad_narrow_buf[0:micro_count].reshape(-1, model_width)
    grad_main, grad_low_w = lax.cond(
        even_section, attention_weights, feed_weights, left_in, left_mid, wide_rows, narrow_rows
    )
    grad_bias = jnp.sum(wide_rows, axis=0, dtype=jnp.float32)
    summed_grads = (
        lax.psum_scatter(grad_main, "dp", scatter_dimension=0, tiled=True),
        lax.psum_scatter(grad_low_w, "dp", scatter_dimension=0, tiled=True),
        lax.psum_scatter(grad_bias, "dp", scatter_dimension=0, tiled=True),
        lax.psum_scatter(vector_terms, "dp", scatter_dimension=0, tiled=True),
    )
    outgoing = jnp.where(
        section_id == section_count - 1,
        finals[:micro_count],
        jnp.where(section_id == 0, input_grads[:micro_count], jnp.zeros_like(finals[:micro_count])),
    )
    received = lax.all_to_all(outgoing, "section", split_axis=2, concat_axis=0, tiled=True)
    mixed = received[(section_count - 1) * micro_count :]
    input_grad = received[:micro_count]
    return (
        mixed,
        input_grad,
        summed_grads[0][None],
        summed_grads[1][None],
        summed_grads[2][None],
        summed_grads[3][None],
    )


def solution(mesh):
    placed = (
        P(None, "dp", None),
        P(None, "dp"),
        P("section", None, None),
        P("section", None, None),
        P("section", None),
        P("section", None),
        P(None, "dp", None),
    )
    return jax.shard_map(
        on_device,
        mesh=mesh,
        in_specs=placed,
        out_specs=(
            P(None, "dp", "section"),
            P(None, "dp", "section"),
            P("section", "dp", None),
            P("section", "dp", None),
            P("section", "dp"),
            P("section", "dp"),
        ),
        check_vma=False,
    )
```

profile of v0, /device:TPU:1, one launch (start us, length us, event | category | flops | bytes accessed | tf_op | source)
XLA Modules:
  0.0 1067.8 jit_solution(14642045901823778860)
XLA Ops:
  14.9 11.9 %conditional.55 = (f32[512,768]{1,0:T(8,128)S(1)}, bf16[512,768]{1,0:T(8,128)(2,1)}, f32[1,1,12,512]{3,2,1,0:T(8,128)}, f32[512,3072]{0,1:T(8,128)}, bf16[512,3072]{0,1:T(8,128)(2,1)}) conditional(s32[]{:T(128)} %convert_element_type.826, () %tuple.632, (pred[]{:T(512)}, pred[]{:T(512)}, bf16[1,512,768]{2,1,0:T(8,128)(2,1)S(1)}, ...), branch_computations={%region_1.2_spmd, %region_2.12_spmd} | conditional | flops 4852679168 | bytes 216275616 | solution.py:330
  26.8 4.5 collective-permute-start
  37.1 8.9 broadcast_in_dim.676
  46.0 6.8 bitcast_dynamic-update-slice_fusion
  65.0 4.9 bitcast_dynamic-update-slice_fusion.1
  71.9 4.6 fusion.272
  78.0 30.4 %conditional.56 = (bf16[512,768]{1,0:T(8,128)(2,1)}, bf16[1,512,768]{2,1,0:T(8,128)(2,1)}, f32[1,512,768]{2,1,0:T(8,128)S(1)}, f32[1,1,12,512]{3,2,1,0:T(8,128)S...) conditional(s32[]{:T(128)} %convert_element_type.827, () %tuple.634, (pred[]{:T(512)}, ...), branch_computations={%region_13.14_spmd, %region_14.24_spmd} | conditional | flops 4869980672 | bytes 219631376 | solution.py:330
  78.0 18.7 %conditional.76 = (bf16[1,512,768]{2,1,0:T(8,128)(2,1)}, f32[1,512,3072]{2,1,0:T(8,128)}, bf16[1,512,3072]{2,1,0:T(8,128)(2,1)}, f32[1,512,768]{2,1,0:T(8,128)},...) conditional(s32[]{:T(128)} %convert_element_type.698, (bf16[512,768]{1,0:T(8,128)(2,1)}, ...), branch_computations={%region_15.17_spmd, %region_18.23_spmd} | conditional | flops 4869980672 | bytes 194268720
  78.5 5.2 fusion.315
  90.6 4.7 fusion.24
  96.7 6.7 copy.537
  103.4 4.8 copy.539
  110.4 9.5 select_dynamic-update-slice_fusion.3
  125.3 6.1 select_dynamic-update-slice_fusion.12
  131.4 55.4 %collective-permute-done.1 = bf16[512,768]{1,0:T(8,128)(2,1)S(1)} collective-permute-done((bf16[512,768]{1,0:T(8,128)(2,1)}, bf16[512,768]{1,0:T(8,128)(2,1)S(1)}, u32[]{:S(2)}, u32[]{:S(2)}) %collective-permute-start.1) | collective-permute-done | bytes 786464 | tf_op jit(solution)/shard_map/ppermute | solution.py:21
  190.2 29.8 %conditional.57 = (bf16[512,768]{1,0:T(8,128)(2,1)}, bf16[1,512,768]{2,1,0:T(8,128)(2,1)}, f32[1,512,768]{2,1,0:T(8,128)S(1)}, f32[1,1,12,512]{3,2,1,0:T(8,128)S...) conditional(s32[]{:T(128)} %convert_element_type.828, () %tuple.636, (pred[]{:T(512)}, ...), branch_computations={%region_25.26_spmd, %region_26.36_spmd} | conditional | flops 4869980672 | bytes 219631376 | solution.py:330
  190.2 18.1 %conditional.84 = (bf16[1,512,768]{2,1,0:T(8,128)(2,1)}, f32[1,512,3072]{2,1,0:T(8,128)}, bf16[1,512,3072]{2,1,0:T(8,128)(2,1)}, f32[1,512,768]{2,1,0:T(8,128)},...) conditional(s32[]{:T(128)} %convert_element_type.713, (bf16[512,768]{1,0:T(8,128)(2,1)}, ...), branch_computations={%region_27.29_spmd, %region_30.35_spmd} | conditional | flops 4869980672 | bytes 194268720
  190.2 4.8 fusion.316
  201.9 4.7 fusion.42
  208.3 6.7 copy.541
  215.0 4.8 copy.543
  221.9 9.5 select_dynamic-update-slice_fusion.2
  236.8 6.1 select_dynamic-update-slice_fusion.11
  246.1 15.7 %conditional.58 = (bf16[512,768]{1,0:T(8,128)(2,1)}, bf16[1,512,768]{2,1,0:T(8,128)(2,1)}, f32[1,512,768]{2,1,0:T(8,128)S(1)}, f32[1,1,12,512]{3,2,1,0:T(8,128)S...) conditional(s32[]{:T(128)} %convert_element_type.829, () %tuple.638, (pred[]{:T(512)}, ...), branch_computations={%region_37.38_spmd, %region_38.48_spmd} | conditional | flops 4869980672 | bytes 219631376 | solution.py:330
  261.8 38.6 %collective-permute-start.3 = (bf16[512,768]{1,0:T(8,128)(2,1)}, bf16[512,768]{1,0:T(8,128)(2,1)S(1)}, u32[]{:S(2)}, u32[]{:S(2)}) collective-permute-start(bf16[512,768]{1,0:T(8,128)(2,1)} %get-tuple-element.2861), channel_id=1, source_target_pairs={{0,8},{8,16},{16,24},{1,9},{9,17},{17,25},{2,10},{10,18},{18,26},{... | collective-permute-start | bytes 2359304 | tf_op jit(solution)/shard_map/ppermute | solution.py:21
  300.4 9.3 select_dynamic-update-slice_fusion.1
  315.0 6.0 select_dynamic-update-slice_fusion.10
  324.3 14.0 %conditional.59 = (bf16[1,512,768]{2,1,0:T(8,128)(2,1)}, f32[1,512,768]{2,1,0:T(8,128)}, f32[1,1,12,512]{3,2,1,0:T(8,128)S(1)}, f32[1,512,3072]{1,2,0:T(8,128)}, bf16[1,512,3072]{1,2,0:T(8,128)(2,1)S(1)}) conditional(s32[]{:T(128)} %convert_element_type.830, () %tuple.640, (pred[]{:T(512)}, bf16[512,768]{1,0:T(8,128)(2,1)}, ...), branch_computations={%region_49.50_spmd, %region_50.0_spmd} | conditional | flops 4866441728 | bytes 214017696 | solution.py:330
  338.4 5.2 select_dynamic-update-slice_fusion.9
  343.5 5.8 slice.1582
  349.3 9.4 select_dynamic-update-slice_fusion
  364.8 11.9 %conditional.60 = (bf16[512,768]{1,0:T(8,128)(2,1)}, f32[2304]{0:T(1024)}, bf16[512,768]{1,0:T(8,128)(2,1)}, bf16[1,512,3072]{1,2,0:T(8,128)(2,1)}) conditional(s32[]{:T(128)} %convert_element_type.831, () %tuple.642, (pred[]{:T(512)}, s32[]{:T(128)}, f32[3,512,768]{2,1,0:T(8,128)}, bf16[2,512,768]{2,1,0:T(8,128)(2,1)}, ...), branch_computations={%region_66.67_spmd, %region_67.86_spmd} | conditional | flops 4874704896 | bytes 199919360 | solution.py:357
  378.6 8.7 copy.505
  398.5 4.6 select_dynamic-update-slice_fusion.8
  403.1 12.3 %conditional.70 = (f32[2304]{0:T(1024)}, bf16[512,768]{1,0:T(8,128)(2,1)}, bf16[1,512,768]{2,1,0:T(8,128)(2,1)}, bf16[1,512,3072]{1,2,0:T(8,128)(2,1)}, bf16[1,512,768]{2,1,0:T(8,128)(2,1)}) conditional(s32[]{:T(128)} %convert_element_type.832, () %tuple.644, (pred[]{:T(512)}, s32[]{:T(128)}, f32[3,512,768]{2,1,0:T(8,128)}, ...), branch_computations={%region_87.88_spmd, %region_88.107_spmd} | conditional | flops 4874704896 | bytes 201492192 | solution.py:357
  420.6 6.1 select_dynamic-update-slice_fusion.7
  426.6 59.3 %collective-permute-done.5 = bf16[512,768]{1,0:T(8,128)(2,1)S(1)} collective-permute-done((bf16[512,768]{1,0:T(8,128)(2,1)}, bf16[512,768]{1,0:T(8,128)(2,1)S(1)}, u32[]{:S(2)}, u32[]{:S(2)}) %collective-permute-start.5) | collective-permute-done | bytes 786464 | tf_op jit(solution)/shard_map/ppermute | solution.py:21
  485.9 56.7 %conditional.71 = (f32[2304]{0:T(1024)}, bf16[512,768]{1,0:T(8,128)(2,1)}, bf16[1,512,768]{2,1,0:T(8,128)(2,1)}, bf16[1,512,3072]{1,2,0:T(8,128)(2,1)}, bf16[1,512,768]{2,1,0:T(8,128)(2,1)}) conditional(s32[]{:T(128)} %convert_element_type.833, () %tuple.646, (pred[]{:T(512)}, s32[]{:T(128)}, f32[3,512,768]{2,1,0:T(8,128)}, ...), branch_computations={%region_108.109_spmd, %region_109.128_spmd} | conditional | flops 4874704896 | bytes 201492192 | solution.py:357
  488.0 47.6 %conditional.88 = (f32[2304]{0:T(1024)}, bf16[1,512,768]{2,1,0:T(8,128)(2,1)}, bf16[1,512,3072]{1,2,0:T(8,128)(2,1)}, bf16[1,512,768]{2,1,0:T(8,128)(2,1)}, bf16[512,768]{1,0:T(8,128)(2,1)}) conditional(s32[]{:T(128)} %convert_element_type.785, (f32[512,768]{1,0:T(8,128)S(1)}, bf16[512,768]{1,0:T(8,128)(2,1)S(1)}, f32[2304]{0:T(1024)S(1)}, ...), branch_computations={%region_110.117_spmd, %region_118.127_spmd} | conditional | flops 4874311680 | bytes 189302272
  492.0 18.7 %copy.529 = f32[3,512,3072]{2,1,0:T(8,128)} copy(f32[3,512,3072]{1,2,0:T(8,128)} %get-tuple-element.3501) | data formatting | bytes 37748736 | tf_op jit(solution)/shard_map
  510.7 9.7 fusion.164
  520.5 4.8 copy.471
  525.3 6.8 add_convert_fusion.22
  547.6 5.9 select_dynamic-update-slice_fusion.6
  553.5 15.1 %collective-permute-done.6 = bf16[512,768]{1,0:T(8,128)(2,1)S(1)} collective-permute-done((bf16[512,768]{1,0:T(8,128)(2,1)}, bf16[512,768]{1,0:T(8,128)(2,1)S(1)}, u32[]{:S(2)}, u32[]{:S(2)}) %collective-permute-start.6) | collective-permute-done | bytes 786464 | tf_op jit(solution)/shard_map/ppermute | solution.py:21
  568.6 56.6 %conditional.72 = (f32[2304]{0:T(1024)}, bf16[512,768]{1,0:T(8,128)(2,1)}, bf16[1,512,768]{2,1,0:T(8,128)(2,1)}, bf16[1,512,3072]{1,2,0:T(8,128)(2,1)}, bf16[1,512,768]{2,1,0:T(8,128)(2,1)}) conditional(s32[]{:T(128)} %convert_element_type.834, () %tuple.648, (pred[]{:T(512)}, s32[]{:T(128)}, f32[3,512,768]{2,1,0:T(8,128)}, ...), branch_computations={%region_129.130_spmd, %region_130.149_spmd} | conditional | flops 4874704896 | bytes 201492192 | solution.py:357
  570.6 47.6 %conditional.89 = (f32[2304]{0:T(1024)}, bf16[1,512,768]{2,1,0:T(8,128)(2,1)}, bf16[1,512,3072]{1,2,0:T(8,128)(2,1)}, bf16[1,512,768]{2,1,0:T(8,128)(2,1)}, bf16[512,768]{1,0:T(8,128)(2,1)}) conditional(s32[]{:T(128)} %convert_element_type.799, (f32[512,768]{1,0:T(8,128)S(1)}, bf16[512,768]{1,0:T(8,128)(2,1)S(1)}, f32[2304]{0:T(1024)S(1)}, ...), branch_computations={%region_131.138_spmd, %region_139.148_spmd} | conditional | flops 4874311680 | bytes 189302272
  574.7 18.7 %copy.530 = f32[3,512,3072]{2,1,0:T(8,128)} copy(f32[3,512,3072]{1,2,0:T(8,128)} %get-tuple-element.3503) | data formatting | bytes 37748736 | tf_op jit(solution)/shard_map
  593.4 9.7 fusion.198
  603.1 4.8 copy.476
  607.9 6.8 add_convert_fusion.28
  630.2 6.0 select_dynamic-update-slice_fusion.5
  638.8 12.8 %conditional.73 = ((f32[2304]{0:T(1024)}, bf16[1,512,768]{2,1,0:T(8,128)(2,1)}, bf16[1,512,3072]{1,2,0:T(8,128)(2,1)}, bf16[1,512,768]{2,1,0:T(8,128)(2,1)})) conditional(s32[]{:T(128)} %convert_element_type.835, () %tuple.650, (pred[]{:T(512)}, s32[]{:T(128)}, f32[3,512,768]{2,1,0:T(8,128)}, bf16[2,512,768]{2,1,0:T(8,128)(2,1)}, ...), branch_computations={%region_150.151_spmd, %region_151.170_spmd} | conditional | flops 4874704896 | bytes 197797472 | solution.py:357
  657.3 6.0 select_dynamic-update-slice_fusion.4
  663.3 5.8 slice.1581
  669.2 8.8 copy.504
  677.9 18.1 %conditional.74 = (f32[768,3072]{1,0:T(8,128)}, f32[3072,768]{1,0:T(8,128)}) conditional(s32[]{:T(128)} %convert_element_type.836, (bf16[1024,768]{1,0:T(8,128)(2,1)S(1)}, bf16[1024,3072]{1,0:T(8,128)(2,1)}, bf16[1024,3072]{1,0:T(8,128)(2,1)}, bf16[1024,768]{1,0:T(8,128)(2,1)}) %tuple.1017, (bf16[1024,3072]{1,0:T(8,128)(2,1)}, ...), branch_computations={%region_170.171_spmd, %region_171.172_spmd} | conditional | flops 9663676416 | bytes 66060360 | solution.py:371
  677.9 10.5 fusion.313
  688.4 7.6 fusion.314
  717.7 4.9 copy.502
  722.7 36.5 %all-to-all-start = ((bf16[2,512,768]{1,0,2:T(2,128)(2,1)}), bf16[2,512,768]{1,0,2:T(2,128)(2,1)S(1)}, u32[]{:S(2)}, u32[]{:S(2)}) async-start(bf16[2,512,768]{1,0,2:T(2,128)(2,1)} %copy.502), calls=%async_computation | async-start | bytes 3145728 | tf_op jit(solution)/shard_map/all_to_all | solution.py:386
  765.7 33.7 %all-reduce.7 = (f32[3072]{0:T(1024)S(1)}, f32[2304]{0:T(1024)S(1)}) all-reduce(f32[3072]{0:T(1024)S(1)} %convert_reduce_fusion.20, f32[2304]{0:T(1024)S(1)} %add_add_fusion.10), channel_id=4, replica_groups=mesh['section'=4,'dp'=8] {'dp'}, use_global_device_ids=true, to_apply=%region_175.176.clone | all-reduce | flops 5376 | bytes 43008
  801.8 92.1 %reduce-scatter.3.cloned.1.call-done = f32[96,3072]{1,0:T(8,128)} async-done(((f32[768,3072]{1,0:T(8,128)}), f32[96,3072]{1,0:T(8,128)}) %reduce-scatter.3.cloned.1.call-update) | async-done | bytes 1179664 | tf_op jit(solution)/shard_map/reduce_scatter | solution.py:376
  894.0 166.6 %reduce-scatter.5.cloned.1.call-done = f32[384,768]{1,0:T(8,128)} async-done(((f32[3072,768]{1,0:T(8,128)}), f32[384,768]{1,0:T(8,128)}) %reduce-scatter.5.cloned.1.call-update) | async-done | bytes 1179664 | tf_op jit(solution)/shard_map/reduce_scatter | solution.py:377
  (214 shorter events, 195.7 us)
Async XLA Ops:
  7.2 6.8 copy-start.102
  7.2 6.8 copy-start.106
  7.2 886.8 %reduce-scatter.3.cloned.1.call-start = ((), (), s32[]{:S(2)}) async-start(), calls=%async_computation.3 | async-start | bytes 10616832 | tf_op jit(solution)/shard_map/reduce_scatter | solution.py:376
  14.0 0.9 copy-start.37
  26.8 45.0 %collective-permute-start = (bf16[512,768]{1,0:T(8,128)(2,1)}, bf16[512,768]{1,0:T(8,128)(2,1)}, u32[]{:S(2)}, u32[]{:S(2)}) collective-permute-start(bf16[512,768]{1,0:T(8,128)(2,1)} %get-tuple-element.2855), channel_id=1, source_target_pairs={{0,8},{8,16},{16,24},{1,9},{9,17},{17,25},{2,10},{10,18},{18,26},{... | collective-permute-start | bytes 2359304 | tf_op jit(solution)/shard_map/ppermute | solution.py:21
  52.8 7.1 copy-start.115
  65.0 7.0 copy-start.20
  76.6 1.4 copy-start.17
  78.5 5.3 copy-start.70
  78.5 5.3 copy-start.103
  78.5 5.3 copy-start.117
  87.8 2.7 copy-start
  96.7 6.7 copy-start.93
  103.4 4.8 copy-start.2
  103.4 4.8 copy-start.94
  108.5 78.4 %collective-permute-start.1 = (bf16[512,768]{1,0:T(8,128)(2,1)}, bf16[512,768]{1,0:T(8,128)(2,1)S(1)}, u32[]{:S(2)}, u32[]{:S(2)}) collective-permute-start(bf16[512,768]{1,0:T(8,128)(2,1)} %get-tuple-element.2857), channel_id=1, source_target_pairs={{0,8},{8,16},{16,24},{1,9},{9,17},{17,25},{2,10},{10,18},{18,26},{... | collective-permute-start | bytes 2359304 | tf_op jit(solution)/shard_map/ppermute | solution.py:21
  190.2 4.8 copy-start.65
  190.2 4.8 copy-start.104
  190.2 4.9 copy-start.118
  199.1 2.8 copy-start.3
  208.3 6.7 copy-start.95
  215.0 4.8 copy-start.5
  215.0 4.8 copy-start.96
  220.0 22.9 %collective-permute-start.2 = (bf16[512,768]{1,0:T(8,128)(2,1)}, bf16[512,768]{1,0:T(8,128)(2,1)S(1)}, u32[]{:S(2)}, u32[]{:S(2)}) collective-permute-start(bf16[512,768]{1,0:T(8,128)(2,1)} %get-tuple-element.2859), channel_id=1, source_target_pairs={{0,8},{8,16},{16,24},{1,9},{9,17},{17,25},{2,10},{10,18},{18,26},{... | collective-permute-start | bytes 2359304 | tf_op jit(solution)/shard_map/ppermute | solution.py:21
  261.8 59.3 %collective-permute-start.3 = (bf16[512,768]{1,0:T(8,128)(2,1)}, bf16[512,768]{1,0:T(8,128)(2,1)S(1)}, u32[]{:S(2)}, u32[]{:S(2)}) collective-permute-start(bf16[512,768]{1,0:T(8,128)(2,1)} %get-tuple-element.2861), channel_id=1, source_target_pairs={{0,8},{8,16},{16,24},{1,9},{9,17},{17,25},{2,10},{10,18},{18,26},{... | collective-permute-start | bytes 2359304 | tf_op jit(solution)/shard_map/ppermute | solution.py:21
  338.3 5.2 copy-start.100
  358.7 3.9 copy-start.101
  358.7 6.1 copy-start.38
  376.7 26.5 %collective-permute-start.4 = (bf16[512,768]{1,0:T(8,128)(2,1)}, bf16[512,768]{1,0:T(8,128)(2,1)S(1)}, u32[]{:S(2)}, u32[]{:S(2)}) collective-permute-start(bf16[512,768]{1,0:T(8,128)(2,1)} %get-tuple-element.2883), channel_id=1, source_target_pairs={{8,0},{16,8},{24,16},{9,1},{17,9},{25,17},{10,2},{18,10},{26,18},{... | collective-permute-start | bytes 2359304 | tf_op jit(solution)/shard_map/ppermute | solution.py:21
  415.5 70.5 %collective-permute-start.5 = (bf16[512,768]{1,0:T(8,128)(2,1)}, bf16[512,768]{1,0:T(8,128)(2,1)S(1)}, u32[]{:S(2)}, u32[]{:S(2)}) collective-permute-start(bf16[512,768]{1,0:T(8,128)(2,1)} %get-tuple-element.2885), channel_id=1, source_target_pairs={{8,0},{16,8},{24,16},{9,1},{17,9},{25,17},{10,2},{18,10},{26,18},{... | collective-permute-start | bytes 2359304 | tf_op jit(solution)/shard_map/ppermute | solution.py:21
  485.9 1.9 copy-start.23
  489.8 1.1 copy-start.52
  520.5 4.8 copy-start.53
  542.7 25.9 %collective-permute-start.6 = (bf16[512,768]{1,0:T(8,128)(2,1)}, bf16[512,768]{1,0:T(8,128)(2,1)S(1)}, u32[]{:S(2)}, u32[]{:S(2)}) collective-permute-start(bf16[512,768]{1,0:T(8,128)(2,1)} %get-tuple-element.2887), channel_id=1, source_target_pairs={{8,0},{16,8},{24,16},{9,1},{17,9},{25,17},{10,2},{18,10},{26,18},{... | collective-permute-start | bytes 2359304 | tf_op jit(solution)/shard_map/ppermute | solution.py:21
  568.6 1.9 copy-start.24
  572.4 1.1 copy-start.54
  603.1 4.8 copy-start.55
  625.2 13.5 %collective-permute-start.7 = (bf16[512,768]{1,0:T(8,128)(2,1)}, bf16[512,768]{1,0:T(8,128)(2,1)S(1)}, u32[]{:S(2)}, u32[]{:S(2)}) collective-permute-start(bf16[512,768]{1,0:T(8,128)(2,1)} %get-tuple-element.2889), channel_id=1, source_target_pairs={{8,0},{16,8},{24,16},{9,1},{17,9},{25,17},{10,2},{18,10},{26,18},{... | collective-permute-start | bytes 2359304 | tf_op jit(solution)/shard_map/ppermute | solution.py:21
  669.2 8.8 copy-start.80
  677.9 10.5 copy-start.39
  677.9 10.5 copy-start.81
  696.1 364.5 %reduce-scatter.5.cloned.1.call-start = ((), (), s32[]{:S(2)}) async-start(), calls=%async_computation.4 | async-start | bytes 10616832 | tf_op jit(solution)/shard_map/reduce_scatter | solution.py:377
  696.4 1.7 copy-start.18
  717.7 41.5 %copy-start.121 = (u32[32]{0:T(128)S(1)}, u32[32]{0:T(128)}, u32[]{:S(2)}) copy-start(u32[32]{0:T(128)} %constant.2020) | copy-start | bytes 388
  722.7 78.0 %all-to-all-start = ((bf16[2,512,768]{1,0,2:T(2,128)(2,1)}), bf16[2,512,768]{1,0,2:T(2,128)(2,1)S(1)}, u32[]{:S(2)}, u32[]{:S(2)}) async-start(bf16[2,512,768]{1,0,2:T(2,128)(2,1)} %copy.502), calls=%async_computation | async-start | bytes 3145728 | tf_op jit(solution)/shard_map/all_to_all | solution.py:386
Sparse Core Ops, SparseCore 0:
  696.2 197.7 reduce-scatter.2
  898.1 162.3 reduce-scatter.4
where the time goes:
time: 1080 us; the launch traced here: 1070 us
  waiting for transfers between devices  393 us (36%)
  other arithmetic  214 us (20%)
  local copies, waits for them, and re-layouts  185 us (17%)
  starting transfers between devices  91.5 us (8%)
  matrix products  69.4 us (6%)
  loops' own time  64.3 us (6%)
  blocking collectives  33.7 us (3%)
  between operations  16.2 us (2%)
    reduce_scatter x1, waiting for transfers between devices, on_device(): lax.psum_scatter(grad_low_w, 'dp', scatter_dimension=0, tiled=True)  167 us
    ppermute x8, waiting for transfers between devices, passed_along(): return lax.ppermute(block, axis, route)  134 us
    reduce_scatter x1, waiting for transfers between devices, on_device(): lax.psum_scatter(grad_main, 'dp', scatter_dimension=0, tiled=True)  92.1 us
    another operation x40, local copies, waits for them, and re-layouts  83.9 us
    ppermute x8, starting transfers between devices, passed_along(): return lax.ppermute(block, axis, route)  54.7 us
    scatter x5, other arithmetic, on_device(): kept_wide = kept_wide.at[store_slot].set(kept_state[0])  44.5 us
    another operation x5, loops' own time, on_device(): lax.cond(active_tick, run_backward, spare_backward, segment_ids[read_slot...  37.1 us
    all_to_all x1, starting transfers between devices, on_device(): lax.all_to_all(outgoing, 'section', split_axis=2, concat_axis=0, tiled=True)  36.5 us
  transfers between devices with their start and end apart: 11, of which 7 were waited for; matrix products, arithmetic and copies ran while one was open for 17% of the time, Pallas kernels for 0%

commit v1 on v0

v1 whole, which is shorter than its diff:
```python
import functools
import math

import jax
import jax.numpy as jnp
from jax import lax
from jax.experimental import pallas as pl
from jax.experimental.pallas import tpu as pltpu
from jax.sharding import PartitionSpec as P

D = 768
HEADS = 12
HEAD_DIM = 64
FF = 3072
BLK = 512
MICRO = 2
CH = 256
GROUP = 8
EPS = 1e-06
NEG = -1e30
K0 = math.sqrt(2.0 / math.pi)
K1 = K0 * 0.044715
MIB = 1 << 20
bf16, f32 = jnp.bfloat16, jnp.float32
MESH = pl.DeviceIdType.MESH
NN = (((1,), (0,)), ((), ()))
NT = (((1,), (1,)), ((), ()))
TN = (((0,), (0,)), ((), ()))
TT = (((0,), (1,)), ((), ()))
PARTS_IN = ((0, 2304, (0, 1, 2)), (2304, 768, (1, 0, 2)))
PARTS_DOWN = ((0, 512, (0, 1, 2)), (512, 256, (1, 0, 2)))


def dot(a, b, dims):
    return lax.dot_general(a, b, dims, preferred_element_type=f32)


def bit(value, b):
    return (value // (1 << b)) % 2


def chunks(me, order, step, flip):
    base = sum(bit(me, order[i]) * (1 << order[i]) for i in range(step))
    own = bit(me, order[step])
    base = base + ((1 - own) if flip else own) * (1 << order[step])
    free = order[step + 1 :]
    out = []
    for k in range(1 << len(free)):
        out.append(base + sum(((k >> i) & 1) << free[i] for i in range(len(free))))
    return out


FIRST_SLOT = (0, 4, 6)


def kernel(
    low,
    inputs,
    seg,
    w_in,
    w_down,
    vec_in,
    vec_out,
    cotangent,
    mixed,
    in_grad,
    out_in,
    out_down,
    out_vec,
    wi,
    wd,
    a_buf,
    d_buf,
    y_buf,
    e_buf,
    q_buf,
    p_buf,
    xh,
    rstd,
    bias,
    rope,
    inv,
    bias_t,
    dw,
    dv,
    split,
    acc,
    db,
    vec_send,
    vec_recv,
    w_sem,
    load_sem,
    fwd_send,
    fwd_recv,
    bwd_send,
    bwd_recv,
    mix_send,
    mix_recv,
    grad_recv,
    vec_ssem,
    vec_rsem,
    free_sem,
    rs_send,
    rs_recv,
    out_sem,
):
    sec = lax.axis_index("section")
    dp = lax.axis_index("dp")
    me = dp // low
    even = sec % 2 == 0
    odd = sec % 2 == 1

    def peer(b):
        return dp + (1 - 2 * bit(me, b)) * (1 << b) * low

    load_wi = pltpu.make_async_copy(w_in.at[0], wi, w_sem.at[0])
    load_wd = pltpu.make_async_copy(w_down.at[0], wd, w_sem.at[1])

    def load_a(m):
        return pltpu.make_async_copy(inputs.at[m], a_buf.at[m], load_sem.at[m])

    def load_d(m):
        return pltpu.make_async_copy(cotangent.at[m], d_buf.at[m], load_sem.at[m])

    @pl.when(sec == 0)
    def _():
        for m in range(MICRO):
            load_a(m).start()

    load_wi.start()

    @pl.when(odd)
    def _():
        load_wd.start()

    @pl.when(sec == 3)
    def _():
        for m in range(MICRO):
            load_d(m).start()

    barrier = pltpu.get_barrier_semaphore()
    for k in range(1, 4):
        pl.semaphore_signal(barrier, inc=1, device_id={"section": (sec + k) % 4}, device_id_type=MESH)
    for k in range(1, GROUP):
        pl.semaphore_signal(barrier, inc=1, device_id={"dp": (dp + k * low) % (GROUP * low)}, device_id_type=MESH)

    acc[...] = jnp.zeros_like(acc)
    db[...] = jnp.zeros_like(db)

    def clear(i, _):
        rows = pl.ds(pl.multiple_of(i * 96, 96), 96)
        dw[rows, :] = jnp.zeros((96, FF), bf16)
        return 0

    lax.fori_loop(0, 8, clear, 0)

    def clear_down(i, _):
        rows = pl.ds(pl.multiple_of(i * 384, 384), 384)
        dv[rows, :] = jnp.zeros((384, D), bf16)
        return 0

    @pl.when(odd)
    def _():
        lax.fori_loop(0, 8, clear_down, 0)

    def rows_of(c):
        return pl.ds(pl.multiple_of(c * CH, CH), CH)

    def forward_copy(m, c):
        rows = rows_of(c)
        return pltpu.make_async_remote_copy(
            src_ref=y_buf.at[m, rows],
            dst_ref=a_buf.at[m, rows],
            send_sem=fwd_send.at[m, c],
            recv_sem=fwd_recv.at[m, c],
            device_id={"section": sec + 1},
            device_id_type=MESH,
        )

    def backward_copy(m, c):
        rows = rows_of(c)
        return pltpu.make_async_remote_copy(
            src_ref=d_buf.at[m, rows],
            dst_ref=d_buf.at[m, rows],
            send_sem=bwd_send.at[m, c],
            recv_sem=bwd_recv.at[m, c],
            device_id={"section": sec - 1},
            device_id_type=MESH,
        )

    def share_copy(m, c, k, out, recv):
        rows = rows_of(c)
        return pltpu.make_async_remote_copy(
            src_ref=split.at[k, m, rows],
            dst_ref=out.at[m, rows],
            send_sem=mix_send.at[k, m, c],
            recv_sem=recv.at[m, c],
            device_id={"section": k},
            device_id_type=MESH,
        )

    def own_copy(m, c, k, out):
        rows = rows_of(c)
        return pltpu.make_async_copy(split.at[k, m, rows], out.at[m, rows], mix_send.at[k, m, c])

    def share(m, c, value, own, out, recv):
        for k in range(4):
            split[k, m, rows_of(c), :] = value[:, 192 * k : 192 * (k + 1)]
        for k in range(4):
            if k == own:
                own_copy(m, c, k, out).start()
            else:
                share_copy(m, c, k, out, recv).start()

    def arrive(m, c):
        @pl.when(sec == 0)
        def _():
            @pl.when(c == 0)
            def _():
                load_a(m).wait()

        @pl.when(sec > 0)
        def _():
            forward_copy(m, c).wait_recv()

    def arrive_back(m, c):
        @pl.when(sec == 3)
        def _():
            @pl.when(c == 0)
            def _():
                load_d(m).wait()

        @pl.when(sec < 3)
        def _():
            backward_copy(m, c).wait_recv()

    def finish_forward(m, c, z):
        rows = rows_of(c)
        mean = jnp.mean(z, axis=1, keepdims=True)
        centred = z - mean
        spread = jnp.mean(centred * centred, axis=1, keepdims=True)
        r = lax.rsqrt(spread + EPS)
        unit = centred * r
        xh[m, rows, :] = unit
        rstd[m, rows, :] = r
        y = (unit * vec_out[:, 0:D] + vec_out[:, D : 2 * D]).astype(bf16)

        @pl.when(sec < 3)
        def _():
            y_buf[m, rows, :] = y
            forward_copy(m, c).start()

        @pl.when(sec == 3)
        def _():
            share(m, c, y, 3, mixed, mix_recv)

    def start_backward(m, c):
        rows = rows_of(c)
        dy = d_buf[m, rows, :].astype(f32)
        unit = xh[m, rows, :]
        dyg = dy * vec_out[:, 0:D]
        m1 = jnp.mean(dyg, axis=1, keepdims=True)
        m2 = jnp.mean(dyg * unit, axis=1, keepdims=True)
        dz = rstd[m, rows, :] * (dyg - m1 - unit * m2)
        du = dz.astype(bf16)

        @pl.when(sec < 3)
        def _():
            forward_copy(m, c).wait_send()

        y_buf[m, rows, :] = du
        acc[0:1, :] += jnp.sum(dy * unit, axis=0, keepdims=True)
        acc[1:2, :] += jnp.sum(dy, axis=0, keepdims=True)
        acc[2:3, :] += jnp.sum(du.astype(f32), axis=0, keepdims=True)
        return dz, du

    def finish_backward(m, c, da):
        rows = rows_of(c)

        @pl.when(sec > 0)
        def _():
            d_buf[m, rows, :] = da
            backward_copy(m, c).start()

        @pl.when(sec == 0)
        def _():
            share(m, c, da, 0, in_grad, grad_recv)

    def attention_tables(m):
        row = seg[m].astype(f32)
        column = jnp.concatenate([jnp.broadcast_to(row, (128, BLK)).T] * 4, axis=1)
        same = column == jnp.broadcast_to(row, (BLK, BLK))
        bias[...] = jnp.where(same, 0.0, NEG)
        index = lax.broadcasted_iota(jnp.int32, (BLK, BLK), 0).astype(f32)
        opener = jnp.min(jnp.where(same, index, float(BLK)), axis=0, keepdims=True)
        place = lax.broadcasted_iota(jnp.int32, (1, BLK), 1).astype(f32) - opener
        number = lax.broadcasted_iota(jnp.int32, (HEAD_DIM // 2, BLK), 0).astype(f32)
        angle = place * jnp.exp(number * (-2.0 * math.log(10000.0) / HEAD_DIM))
        rope[m, 0] = jnp.cos(angle)
        rope[m, 1] = jnp.sin(angle)

    def project(m, c):
        arrive(m, c)
        rows = rows_of(c)
        a = a_buf[m, rows, :]
        co, si = rope[m, 0, :, rows], rope[m, 1, :, rows]
        for part in range(3):
            p = dot(wi[:, D * part : D * (part + 1)], a, TT)
            b = bias_t[D * part : D * (part + 1), :]
            p = p + jnp.concatenate([b, b], axis=1)
            if part < 2:
                p4 = p.reshape(HEADS, 2, 32, CH)
                t1, t2 = p4[:, 0], p4[:, 1]
                r1 = t1 * co[None] - t2 * si[None]
                r2 = t2 * co[None] + t1 * si[None]
                if part == 0:
                    r1, r2 = r1 * 0.125, r2 * 0.125
                p = jnp.concatenate([r1[:, None], r2[:, None]], axis=1).reshape(D, CH)
            p = p.astype(bf16)
            for j in range(3):
                q_buf[m, (3 * part + j) * 2 + c] = p[256 * j : 256 * (j + 1), :]

    def both(buf, m, block, rows):
        return jnp.concatenate([buf[m, block * 2, rows, :], buf[m, block * 2 + 1, rows, :]], axis=1)

    def head_forward(m, g, hh):
        h = g * 4 + hh
        rows = slice(64 * hh, 64 * (hh + 1))
        st = dot(both(q_buf, m, 3 + g, rows), both(q_buf, m, g, rows), TN) + bias[...]
        peak = jnp.max(st, axis=0, keepdims=True)
        e = jnp.exp(st - peak)
        total = jnp.sum(e, axis=0, keepdims=True)
        eb = e.astype(bf16)
        e_buf[m, h * 2] = eb[:, 0:256]
        e_buf[m, h * 2 + 1] = eb[:, 256:512]
        r = 1.0 / total
        inv[m, h] = jnp.broadcast_to(r, (8, BLK))
        o = (dot(both(q_buf, m, 6 + g, rows), eb, NN) * r).astype(bf16)
        q_buf[m, (9 + g) * 2, rows, :] = o[:, 0:256]
        q_buf[m, (9 + g) * 2 + 1, rows, :] = o[:, 256:512]

    def heads_forward(m, g):
        for hh in range(4):
            head_forward(m, g, hh)

    def attended(m, c):
        return jnp.concatenate([q_buf[m, (9 + j) * 2 + c] for j in range(3)], axis=0)

    def close(m, c):
        rows = rows_of(c)
        u = dot(attended(m, c), wi[:, 3 * D :], TN) + vec_out[:, 2 * D :]
        finish_forward(m, c, u + a_buf[m, rows, :].astype(f32))

    def attention_forward(m):
        attention_tables(m)

        @pl.when(m == 0)
        def _():
            for i in range(3):
                b = jnp.broadcast_to(vec_in[:, D * i : D * (i + 1)], (128, D))
                bias_t[D * i : D * (i + 1), :] = b.T
            load_wi.wait()

        lax.fori_loop(0, 2, lambda c, _: (project(m, c), 0)[1], 0)
        lax.fori_loop(0, 3, lambda g, _: (heads_forward(m, g), 0)[1], 0)
        lax.fori_loop(0, 2, lambda c, _: (close(m, c), 0)[1], 0)

    def open_back(m, c):
        arrive_back(m, c)
        rows = rows_of(c)
        dz, du = start_backward(m, c)
        xh[m, rows, :] = dz
        do = dot(wi[:, 3 * D :], du, NT).astype(bf16)
        for j in range(3):
            p_buf[m, (9 + j) * 2 + c] = do[256 * j : 256 * (j + 1), :]

    def head_backward(m, g, hh):
        h = g * 4 + hh
        rows = slice(64 * hh, 64 * (hh + 1))
        do = (both(p_buf, m, 9 + g, rows).astype(f32) * inv[m, h, 0:1, :]).astype(bf16)
        o = both(q_buf, m, 9 + g, rows)
        inner = jnp.sum(do.astype(f32) * o.astype(f32), axis=0, keepdims=True)
        e = jnp.concatenate([e_buf[m, h * 2], e_buf[m, h * 2 + 1]], axis=1)
        dr = dot(both(q_buf, m, 6 + g, rows), do, TN)
        ds = e * (dr - inner).astype(bf16)
        dq = dot(both(q_buf, m, 3 + g, rows), ds, NN)
        dk = dot(both(q_buf, m, g, rows), ds, NT)
        dvv = dot(do, e, NT)
        co, si = rope[m, 0], rope[m, 1]
        for part, t in ((0, dq * 0.125), (1, dk)):
            t1, t2 = t[:32], t[32:]
            t = jnp.concatenate([t1 * co + t2 * si, t2 * co - t1 * si], axis=0).astype(bf16)
            p_buf[m, (3 * part + g) * 2, rows, :] = t[:, 0:256]
            p_buf[m, (3 * part + g) * 2 + 1, rows, :] = t[:, 256:512]
        dvv = dvv.astype(bf16)
        p_buf[m, (6 + g) * 2, rows, :] = dvv[:, 0:256]
        p_buf[m, (6 + g) * 2 + 1, rows, :] = dvv[:, 256:512]

    def heads_backward(m, g):
        for hh in range(4):
            head_backward(m, g, hh)

    def close_back(m, c):
        rows = rows_of(c)
        dp_t = jnp.concatenate([p_buf[m, fb * 2 + c] for fb in range(9)], axis=0)
        da = dot(dp_t, wi[:, 0 : 3 * D], TT) + xh[m, rows, :]
        finish_backward(m, c, da.astype(bf16))

    def attention_weights(m):
        a_t = a_buf[m].T

        def part(n, _):
            cols = pl.ds(pl.multiple_of(n * D, D), D)
            d = jnp.concatenate(
                [jnp.concatenate([p_buf[m, (3 * n + j) * 2], p_buf[m, (3 * n + j) * 2 + 1]], axis=1) for j in range(3)],
                axis=0,
            )
            dw[:, cols] = (dw[:, cols].astype(f32) + dot(a_t, d, NT)).astype(bf16)
            db[:, cols] += dot(jnp.ones((8, BLK), bf16), d, NT)
            return 0

        lax.fori_loop(0, 3, part, 0)
        o = jnp.concatenate([attended(m, 0), attended(m, 1)], axis=1)
        dw[:, 3 * D :] = (dw[:, 3 * D :].astype(f32) + dot(o, y_buf[m], NN)).astype(bf16)

    def feed_rows(m, c):
        arrive(m, c)
        rows = rows_of(c)
        a = a_buf[m, rows, :]
        u = None
        for n in range(4):
            cols = slice(D * n, D * (n + 1))
            h = dot(a, wi[:, cols], NN) + vec_in[:, cols]
            h2 = h * h
            s = 0.5 * jnp.tanh(h * (K0 + K1 * h2)) + 0.5
            g = h * s
            slope = (s + g * (1.0 - s) * (2.0 * K0 + 6.0 * K1 * h2)).astype(bf16)
            g = g.astype(bf16)
            for j in range(3):
                q_buf[m, c * 12 + 3 * n + j] = g[:, 256 * j : 256 * (j + 1)]
                e_buf[m, 3 * n + j, rows, :] = slope[:, 256 * j : 256 * (j + 1)]
            t = dot(g, wd[cols, :], NN)
            u = t if u is None else u + t
        finish_forward(m, c, u + vec_out[:, 2 * D :] + a.astype(f32))

    def feed_forward(m):
        @pl.when(m == 0)
        def _():
            load_wi.wait()
            load_wd.wait()

        lax.fori_loop(0, 2, lambda c, _: (feed_rows(m, c), 0)[1], 0)

    def feed_rows_back(m, c):
        arrive_back(m, c)
        rows = rows_of(c)
        dz, du = start_backward(m, c)
        da = dz
        for n in range(4):
            cols = slice(D * n, D * (n + 1))
            dg = dot(du, wd[cols, :], NT)
            slope = jnp.concatenate([e_buf[m, 3 * n + j, rows, :] for j in range(3)], axis=1)
            dh = (dg * slope.astype(f32)).astype(bf16)
            for j in range(3):
                p_buf[m, c * 12 + 3 * n + j] = dh[:, 256 * j : 256 * (j + 1)]
            da = da + dot(dh, wi[:, cols], NT)
        finish_backward(m, c, da.astype(bf16))

    def tile(buf, m, n):
        return jnp.concatenate(
            [jnp.concatenate([buf[m, c * 12 + 3 * n + j] for j in range(3)], axis=1) for c in range(2)], axis=0
        )

    def feed_weights_down(m):
        def part(n, _):
            rows = pl.ds(pl.multiple_of(n * D, D), D)
            dv[rows, :] = (dv[rows, :].astype(f32) + dot(tile(q_buf, m, n), y_buf[m], TN)).astype(bf16)
            return 0

        lax.fori_loop(0, 4, part, 0)

    def feed_weights_in(m):
        def part(n, _):
            cols = pl.ds(pl.multiple_of(n * D, D), D)
            dh = tile(p_buf, m, n)
            dw[:, cols] = (dw[:, cols].astype(f32) + dot(a_buf[m], dh, TN)).astype(bf16)
            db[:, cols] += jnp.broadcast_to(jnp.sum(dh.astype(f32), axis=0, keepdims=True), (8, D))
            return 0

        lax.fori_loop(0, 4, part, 0)

    def part_copy(grad, land, size, number, first, width, order, step, k, j):
        slot = FIRST_SLOT[step] + k
        return pltpu.make_async_remote_copy(
            src_ref=grad.at[pl.ds(pl.multiple_of(j * size, size), size), pl.ds(first, width)],
            dst_ref=land.at[pl.ds(slot * size, size), pl.ds(first, width)],
            send_sem=rs_send.at[number, slot],
            recv_sem=rs_recv.at[number, slot],
            device_id={"dp": peer(order[step])},
            device_id_type=MESH,
        )

    def step_copies(grad, land, size, number, part, step):
        first, width, order = part
        return [
            part_copy(grad, land, size, number, first, width, order, step, k, j)
            for k, j in enumerate(chunks(me, order, step, True))
        ]

    def send_step(*args):
        for copy in step_copies(*args):
            copy.start()

    def take_step(grad, land, size, number, part, step):
        first, width, order = part
        cols = pl.ds(first, width)
        copies = step_copies(grad, land, size, number, part, step)
        for k, j in enumerate(chunks(me, order, step, False)):
            copies[k].wait_recv()
            slot = FIRST_SLOT[step] + k
            rows = pl.ds(pl.multiple_of(j * size, size), size)
            total = grad[rows, cols].astype(f32) + land[slot * size : (slot + 1) * size, cols].astype(f32)
            if step < 2:
                grad[rows, cols] = total.astype(bf16)
        return total

    def wait_sends(grad, land, size, number, part):
        for step in range(3):
            for copy in step_copies(grad, land, size, number, part, step):
                copy.wait_send()

    down_parts = [(dv, wd, 384, i, part) for i, part in enumerate(PARTS_DOWN)]
    in_parts = [(dw, wi, 96, len(PARTS_DOWN) + i, part) for i, part in enumerate(PARTS_IN)]

    def weights_free():
        for b in range(3):
            pl.semaphore_signal(free_sem.at[b], inc=1, device_id={"dp": peer(b)}, device_id_type=MESH)

    def await_free():
        for b in range(3):
            pl.semaphore_wait(free_sem.at[b], 1)

    def attention_backward(m):
        lax.fori_loop(0, 2, lambda c, _: (open_back(m, c), 0)[1], 0)
        lax.fori_loop(0, 3, lambda g, _: (heads_backward(m, g), 0)[1], 0)
        lax.fori_loop(0, 2, lambda c, _: (close_back(m, c), 0)[1], 0)

        @pl.when(m == MICRO - 1)
        def _():
            weights_free()

        attention_weights(m)

    def feed_backward(m):
        lax.fori_loop(0, 2, lambda c, _: (feed_rows_back(m, c), 0)[1], 0)

        @pl.when(m == MICRO - 1)
        def _():
            weights_free()

        begin = jnp.where(sec == 3, 0, m)
        end = jnp.where((sec == 3) & (m == 0), 0, m + 1)
        lax.fori_loop(begin, end, lambda i, _: (feed_weights_down(i), 0)[1], 0)

        @pl.when(m == MICRO - 1)
        def _():
            await_free()
            for p in down_parts:
                send_step(*p, 0)

        lax.fori_loop(begin, end, lambda i, _: (feed_weights_in(i), 0)[1], 0)

    pl.semaphore_wait(barrier, 3 + GROUP - 1)

    def task(t, _):
        forward = jnp.where(sec == 3, t % 2 == 0, t < 2)
        m = jnp.where(sec == 3, t // 2, t % 2)

        @pl.when(forward & even)
        def _():
            attention_forward(m)

        @pl.when(forward & odd)
        def _():
            feed_forward(m)

        @pl.when(jnp.logical_not(forward) & even)
        def _():
            attention_backward(m)

        @pl.when(jnp.logical_not(forward) & odd)
        def _():
            feed_backward(m)

        return 0

    lax.fori_loop(0, 2 * MICRO, task, 0)

    @pl.when(even)
    def _():
        await_free()

    for p in in_parts:
        send_step(*p, 0)

    vec_send[...] = jnp.zeros_like(vec_send)
    outer = jnp.concatenate([acc[0:1, :], acc[1:2, :], acc[2:3, :]], axis=1)
    for j in range(GROUP):
        vec_send[j, 0:1, :] = db[0:1, 384 * j : 384 * (j + 1)]
        vec_send[j, 1:2, 0:288] = outer[:, 288 * j : 288 * (j + 1)]

    def vec_copy(k):
        there = (me + k) % GROUP
        return pltpu.make_async_remote_copy(
            src_ref=vec_send.at[there],
            dst_ref=vec_recv.at[k],
            send_sem=vec_ssem.at[k],
            recv_sem=vec_rsem.at[k],
            device_id={"dp": there * low + dp % low},
            device_id_type=MESH,
        )

    for k in range(1, GROUP):
        vec_copy(k).start()

    for step in range(3):

        @pl.when(odd)
        def _():
            for p in down_parts:
                total = take_step(*p, step)
                if step < 2:
                    send_step(*p, step + 1)
                else:
                    first, width, _ = p[4]
                    xh[1, 0:384, first : first + width] = total

        for p in in_parts:
            total = take_step(*p, step)
            if step < 2:
                send_step(*p, step + 1)
            else:
                first, width, _ = p[4]
                for i in range(width // D):
                    xh[0, 96 * (first // D + i) : 96 * (first // D + i + 1), :] = total[:, D * i : D * (i + 1)]

    @pl.when(even)
    def _():
        xh[1, 0:384, :] = jnp.zeros((384, D), f32)

    outs = [pltpu.make_async_copy(xh.at[1, pl.ds(0, 384)], out_down, out_sem.at[4])]
    for i in range(4):
        outs.append(
            pltpu.make_async_copy(xh.at[0, pl.ds(96 * i, 96)], out_in.at[:, pl.ds(D * i, D)], out_sem.at[i])
        )
    for copy in outs:
        copy.start()
    total = vec_send[me]
    for k in range(1, GROUP):
        vec_copy(k).wait_recv()
        total = total + vec_recv[k]
    out_vec[...] = total

    for k in range(1, GROUP):
        vec_copy(k).wait_send()
    for p in in_parts:
        wait_sends(*p)

    @pl.when(odd)
    def _():
        for p in down_parts:
            wait_sends(*p)

    for m in range(MICRO):
        for c in range(2):

            @pl.when(sec > 0)
            def _():
                backward_copy(m, c).wait_send()
                share_copy(m, c, 0, in_grad, grad_recv).wait_recv()

            @pl.when(sec < 3)
            def _():
                share_copy(m, c, 0, mixed, mix_recv).wait_recv()

            @pl.when(sec == 0)
            def _():
                own_copy(m, c, 0, in_grad).wait()
                for k in range(1, 4):
                    share_copy(m, c, k, in_grad, grad_recv).wait_send()

            @pl.when(sec == 3)
            def _():
                own_copy(m, c, 3, mixed).wait()
                for k in range(3):
                    share_copy(m, c, k, mixed, mix_recv).wait_send()

    for copy in outs:
        copy.wait()


def on_device(inputs, segment_ids, w_in, w_down, vec_in, vec_out, cotangent):
    world = lax.axis_size("dp")
    low = world // GROUP
    hbm = pl.BlockSpec(memory_space=pl.ANY)
    vmem = pl.BlockSpec(memory_space=pltpu.VMEM)
    V, S = pltpu.VMEM, pltpu.SemaphoreType.DMA
    parts = len(PARTS_IN) + len(PARTS_DOWN)
    mixed, in_grad, grad_in, grad_down, grad_vec = pl.pallas_call(
        functools.partial(kernel, low),
        out_shape=(
            jax.ShapeDtypeStruct((MICRO, BLK, D // 4), bf16),
            jax.ShapeDtypeStruct((MICRO, BLK, D // 4), bf16),
            jax.ShapeDtypeStruct((D // GROUP, FF), f32),
            jax.ShapeDtypeStruct((FF // GROUP, D), f32),
            jax.ShapeDtypeStruct((8, 384), f32),
        ),
        in_specs=[hbm, vmem, hbm, hbm, vmem, vmem, hbm],
        out_specs=(hbm, hbm, hbm, hbm, vmem),
        scratch_shapes=[
            V((D, FF), bf16),
            V((FF, D), bf16),
            V((MICRO, BLK, D), bf16),
            V((MICRO, BLK, D), bf16),
            V((MICRO, BLK, D), bf16),
            V((MICRO, 24, 512, 256), bf16),
            V((MICRO, 24, 256, 256), bf16),
            V((MICRO, 24, 256, 256), bf16),
            V((MICRO, BLK, D), f32),
            V((MICRO, BLK, 1), f32),
            V((BLK, BLK), f32),
            V((MICRO, 2, HEAD_DIM // 2, BLK), f32),
            V((MICRO, HEADS, 8, BLK), f32),
            V((3 * D, 128), f32),
            V((D, FF), bf16),
            V((FF, D), bf16),
            V((4, MICRO, BLK, D // 4), bf16),
            V((8, D), f32),
            V((8, FF), f32),
            V((GROUP, 8, 384), f32),
            V((GROUP, 8, 384), f32),
            S((2,)),
            S((MICRO,)),
            S((MICRO, 2)),
            S((MICRO, 2)),
            S((MICRO, 2)),
            S((MICRO, 2)),
            S((4, MICRO, 2)),
            S((MICRO, 2)),
            S((MICRO, 2)),
            S((GROUP,)),
            S((GROUP,)),
            pltpu.SemaphoreType.REGULAR((3,)),
            S((parts, 7)),
            S((parts, 7)),
            S((5,)),
        ],
        compiler_params=pltpu.CompilerParams(
            collective_id=0, has_side_effects=True, vmem_limit_bytes=63 * MIB
        ),
    )(inputs, segment_ids[:, None, :], w_in, w_down, vec_in, vec_out, cotangent)
    vec_a, vec_b = grad_vec[0], grad_vec[1, :288]
    if low > 1:
        groups = [[g * low + i for i in range(low)] for g in range(GROUP)]

        def rest(value):
            return lax.psum_scatter(
                value, "dp", scatter_dimension=0, axis_index_groups=groups, tiled=True
            )

        grad_in, grad_down, vec_a, vec_b = rest(grad_in), rest(grad_down), rest(vec_a), rest(vec_b)
    return mixed, in_grad, grad_in[None], grad_down[None], vec_a[None], vec_b[None]


def solution(mesh):
    placed = (
        P(None, "dp", None),
        P(None, "dp"),
        P("section", None, None),
        P("section", None, None),
        P("section", None),
        P("section", None),
        P(None, "dp", None),
    )
    return jax.shard_map(
        on_device,
        mesh=mesh,
        in_specs=placed,
        out_specs=(
            P(None, "dp", "section"),
            P(None, "dp", "section"),
            P("section", "dp", None),
            P("section", "dp", None),
            P("section", "dp"),
            P("section", "dp"),
        ),
        check_vma=False,
    )
```

time: 1080 us -> 227 us (0.21); the launches traced: 1070 us -> 226 us
  waiting for transfers between devices: 393 us -> 0 us
  Pallas kernels: 0 us -> 216 us
  other arithmetic: 214 us -> 0 us
  local copies, waits for them, and re-layouts: 185 us -> 10 us
  starting transfers between devices: 91.5 us -> 0 us
  matrix products: 69.4 us -> 0 us
  loops' own time: 64.3 us -> 0 us
  blocking collectives: 33.7 us -> 0 us
  between operations: 16.2 us -> 0.65 us
    reduce_scatter x2 -> x0, waiting for transfers between devices: 259 us -> none  [the longest x1 167 us: on_device(): lax.psum_scatter(grad_low_w, 'dp', scatter_dimension=0, tiled=True)]
    pallas_call x0 -> x1, Pallas kernels: none -> 216 us  [on_device(): pl.pallas_call(functools.partial(kernel, low), out_shape=(jax.ShapeDtypeS...]
    scatter x44 -> x0, other arithmetic: 178 us -> none  [the longest x5 44.5 us: on_device(): kept_wide = kept_wide.at[store_slot].set(kept_state[0])]
    ppermute x8 -> x0, waiting for transfers between devices: 134 us -> none  [passed_along(): return lax.ppermute(block, axis, route)]
    another operation x40 -> x0, local copies, waits for them, and re-layouts: 83.9 us -> none
    dot_general x10 -> x0, matrix products: 69.4 us -> none  [the longest x2 19.5 us: feed_backward(): lax.dot_general(grad_branch, w_low, CONTRACT_COLS, preferred_element_type...]
    another operation x11 -> x0, loops' own time: 58.9 us -> none  [the longest x5 37.1 us: on_device(): lax.cond(active_tick, run_backward, spare_backward, segment_ids[read_slot...]
    ppermute x8 -> x0, starting transfers between devices: 54.7 us -> none  [passed_along(): return lax.ppermute(block, axis, route)]
  transfers between devices with their start and end apart: 11 -> 0, of which waited for: 7 -> 0; matrix products, arithmetic and copies ran while one was open for 17% -> 0% of each run, Pallas kernels for 0% -> 0%
where the time goes in v1:
time: 227 us; the launch traced here: 226 us
  Pallas kernels  216 us (95%)
  local copies, waits for them, and re-layouts  10 us (4%)
    pallas_call x1, Pallas kernels, on_device(): pl.pallas_call(functools.partial(kernel, low), out_shape=(jax.ShapeDtypeS...  216 us
    unnamed x8, local copies, waits for them, and re-layouts  6.19 us

profile of v1, /device:TPU:1, one launch (start us, length us, event | category | flops | bytes accessed | tf_op | source)
XLA Modules:
  0.0 226.4 jit_solution(9717640578574389302)
XLA Ops:
  0.6 1.3 broadcast_in_dim.9.seg
  1.9 215.7 %shard_map.118 = (bf16[2,512,192]{2,1,0:T(8,128)(2,1)}, bf16[2,512,192]{2,1,0:T(8,128)(2,1)}, f32[96,3072]{1,0:T(8,128)}, f32[384,768]{1,0:T(8,128)}, f32[8,384]{1,0:T(8,128)}) custom-call(bf16[2,512,768]{2,1,0:T(8,128)(2,1)} %inputs.1, s32[2,1,512]{2,1,0:T(1,128)} %broadcast_in_dim.9.seg, bf16[1,768,3072]{2,1,0:T(8,128)(2,1)} %w_in.1, ...), custom_call_target="tpu_custom_call" | custom-call | tf_op jit(solution)/shard_map/pallas_call | solution.py:709
  217.6 0.0 copy-start.1
  217.7 2.1 copy.13
  219.7 1.3 slice.7
  221.0 1.3 slice.6
  222.3 0.0 copy-start
  222.3 2.1 copy.14
  224.4 0.0 copy-done.1
  224.4 1.0 copy.17
  225.4 0.0 copy-done
  225.4 1.0 copy.18
Async XLA Ops:
  217.6 6.7 %copy-start.1 = (f32[96,3072]{1,0:T(8,128)S(1)}, f32[96,3072]{1,0:T(8,128)}, u32[]{:S(2)}) copy-start(f32[96,3072]{1,0:T(8,128)} %get-tuple-element.13) | copy-start | bytes 3538948
  222.3 3.1 %copy-start = (f32[384,768]{1,0:T(8,128)S(1)}, f32[384,768]{1,0:T(8,128)}, u32[]{:S(2)}) copy-start(f32[384,768]{1,0:T(8,128)} %get-tuple-element.14) | copy-start | bytes 3538948

commit v2 on v1

--- a/solution.py
+++ b/solution.py
@@ -27,8 +27,9 @@
 NT = (((1,), (1,)), ((), ()))
 TN = (((0,), (0,)), ((), ()))
 TT = (((0,), (1,)), ((), ()))
-PARTS_IN = ((0, 2304, (0, 1, 2)), (2304, 768, (1, 0, 2)))
-PARTS_DOWN = ((0, 512, (0, 1, 2)), (512, 256, (1, 0, 2)))
+ORDER_A, ORDER_B = (0, 1, 2), (1, 0, 2)
+DOWN_PARTS = [(True, 128 * i, 128, ORDER_A if i % 3 else ORDER_B) for i in range(6)]
+IN_PARTS = [(False, 256 * i, 256, ORDER_A if i % 3 else ORDER_B) for i in range(12)]
 
 
 def dot(a, b, dims):
@@ -51,6 +52,9 @@
 
 
 FIRST_SLOT = (0, 4, 6)
+PARTS = DOWN_PARTS + IN_PARTS
+DOWN = list(range(len(DOWN_PARTS)))
+IN = list(range(len(DOWN_PARTS), len(PARTS)))
 
 
 def kernel(
@@ -66,7 +70,8 @@
     in_grad,
     out_in,
     out_down,
-    out_vec,
+    out_vec_in,
+    out_vec_out,
     wi,
     wd,
     a_buf,
@@ -147,22 +152,6 @@
     acc[...] = jnp.zeros_like(acc)
     db[...] = jnp.zeros_like(db)
 
-    def clear(i, _):
-        rows = pl.ds(pl.multiple_of(i * 96, 96), 96)
-        dw[rows, :] = jnp.zeros((96, FF), bf16)
-        return 0
-
-    lax.fori_loop(0, 8, clear, 0)
-
-    def clear_down(i, _):
-        rows = pl.ds(pl.multiple_of(i * 384, 384), 384)
-        dv[rows, :] = jnp.zeros((384, D), bf16)
-        return 0
-
-    @pl.when(odd)
-    def _():
-        lax.fori_loop(0, 8, clear_down, 0)
-
     def rows_of(c):
         return pl.ds(pl.multiple_of(c * CH, CH), CH)
 
@@ -189,10 +178,10 @@
         )
 
     def share_copy(m, c, k, out, recv):
-        rows = rows_of(c)
+        cols = rows_of(c)
         return pltpu.make_async_remote_copy(
-            src_ref=split.at[k, m, rows],
-            dst_ref=out.at[m, rows],
+            src_ref=split.at[k, m, :, cols],
+            dst_ref=out.at[m, :, cols],
             send_sem=mix_send.at[k, m, c],
             recv_sem=recv.at[m, c],
             device_id={"section": k},
@@ -200,12 +189,13 @@
         )
 
     def own_copy(m, c, k, out):
-        rows = rows_of(c)
-        return pltpu.make_async_copy(split.at[k, m, rows], out.at[m, rows], mix_send.at[k, m, c])
+        cols = rows_of(c)
+        return pltpu.make_async_copy(split.at[k, m, :, cols], out.at[m, :, cols], mix_send.at[k, m, c])
 
     def share(m, c, value, own, out, recv):
+        flipped = value.T
         for k in range(4):
-            split[k, m, rows_of(c), :] = value[:, 192 * k : 192 * (k + 1)]
+            split[k, m, :, rows_of(c)] = flipped[192 * k : 192 * (k + 1), :]
         for k in range(4):
             if k == own:
                 own_copy(m, c, k, out).start()
@@ -272,7 +262,8 @@
         acc[0:1, :] += jnp.sum(dy * unit, axis=0, keepdims=True)
         acc[1:2, :] += jnp.sum(dy, axis=0, keepdims=True)
         acc[2:3, :] += jnp.sum(du.astype(f32), axis=0, keepdims=True)
-        return dz, du
+        xh[m, rows, :] = dz
+        return du
 
     def finish_backward(m, c, da):
         rows = rows_of(c)
@@ -287,7 +278,7 @@
             share(m, c, da, 0, in_grad, grad_recv)
 
     def attention_tables(m):
-        row = seg[m].astype(f32)
+        row = seg[pl.ds(m, 1), :].astype(f32)
         column = jnp.concatenate([jnp.broadcast_to(row, (128, BLK)).T] * 4, axis=1)
         same = column == jnp.broadcast_to(row, (BLK, BLK))
         bias[...] = jnp.where(same, 0.0, NEG)
@@ -323,25 +314,30 @@
     def both(buf, m, block, rows):
         return jnp.concatenate([buf[m, block * 2, rows, :], buf[m, block * 2 + 1, rows, :]], axis=1)
 
-    def head_forward(m, g, hh):
-        h = g * 4 + hh
-        rows = slice(64 * hh, 64 * (hh + 1))
-        st = dot(both(q_buf, m, 3 + g, rows), both(q_buf, m, g, rows), TN) + bias[...]
-        peak = jnp.max(st, axis=0, keepdims=True)
-        e = jnp.exp(st - peak)
-        total = jnp.sum(e, axis=0, keepdims=True)
-        eb = e.astype(bf16)
-        e_buf[m, h * 2] = eb[:, 0:256]
-        e_buf[m, h * 2 + 1] = eb[:, 256:512]
-        r = 1.0 / total
-        inv[m, h] = jnp.broadcast_to(r, (8, BLK))
-        o = (dot(both(q_buf, m, 6 + g, rows), eb, NN) * r).astype(bf16)
-        q_buf[m, (9 + g) * 2, rows, :] = o[:, 0:256]
-        q_buf[m, (9 + g) * 2 + 1, rows, :] = o[:, 256:512]
-
-    def heads_forward(m, g):
-        for hh in range(4):
-            head_forward(m, g, hh)
+    def heads_forward(m):
+        scores, weights = {}, {}
+        for t in range(HEADS + 2):
+            if t < HEADS:
+                g, rows = t // 4, slice(64 * (t % 4), 64 * (t % 4) + 64)
+                scores[t] = dot(both(q_buf, m, 3 + g, rows), both(q_buf, m, g, rows), TN) + bias[...]
+            h = t - 1
+            if 0 <= h < HEADS:
+                st = scores.pop(h)
+                peak = jnp.max(st, axis=0, keepdims=True)
+                e = jnp.exp(st - peak)
+                r = 1.0 / jnp.sum(e, axis=0, keepdims=True)
+                e = e.astype(bf16)
+                e_buf[m, h * 2] = e[:, 0:256]
+                e_buf[m, h * 2 + 1] = e[:, 256:512]
+                inv[m, h] = jnp.broadcast_to(r, (8, BLK))
+                weights[h] = (e, r)
+            h = t - 2
+            if 0 <= h:
+                e, r = weights.pop(h)
+                g, rows = h // 4, slice(64 * (h % 4), 64 * (h % 4) + 64)
+                o = (dot(both(q_buf, m, 6 + g, rows), e, NN) * r).astype(bf16)
+                q_buf[m, (9 + g) * 2, rows, :] = o[:, 0:256]
+                q_buf[m, (9 + g) * 2 + 1, rows, :] = o[:, 256:512]
 
     def attended(m, c):
         return jnp.concatenate([q_buf[m, (9 + j) * 2 + c] for j in range(3)], axis=0)
@@ -352,59 +348,62 @@
         finish_forward(m, c, u + a_buf[m, rows, :].astype(f32))
 
     def attention_forward(m):
-        attention_tables(m)
-
         @pl.when(m == 0)
         def _():
-            for i in range(3):
-                b = jnp.broadcast_to(vec_in[:, D * i : D * (i + 1)], (128, D))
-                bias_t[D * i : D * (i + 1), :] = b.T
             load_wi.wait()
 
+        @pl.when(m > 0)
+        def _():
+            attention_tables(m)
+
         lax.fori_loop(0, 2, lambda c, _: (project(m, c), 0)[1], 0)
-        lax.fori_loop(0, 3, lambda g, _: (heads_forward(m, g), 0)[1], 0)
+        heads_forward(m)
         lax.fori_loop(0, 2, lambda c, _: (close(m, c), 0)[1], 0)
 
     def open_back(m, c):
         arrive_back(m, c)
         rows = rows_of(c)
-        dz, du = start_backward(m, c)
-        xh[m, rows, :] = dz
+        du = start_backward(m, c)
         do = dot(wi[:, 3 * D :], du, NT).astype(bf16)
         for j in range(3):
             p_buf[m, (9 + j) * 2 + c] = do[256 * j : 256 * (j + 1), :]
 
-    def head_backward(m, g, hh):
-        h = g * 4 + hh
-        rows = slice(64 * hh, 64 * (hh + 1))
-        do = (both(p_buf, m, 9 + g, rows).astype(f32) * inv[m, h, 0:1, :]).astype(bf16)
-        o = both(q_buf, m, 9 + g, rows)
-        inner = jnp.sum(do.astype(f32) * o.astype(f32), axis=0, keepdims=True)
-        e = jnp.concatenate([e_buf[m, h * 2], e_buf[m, h * 2 + 1]], axis=1)
-        dr = dot(both(q_buf, m, 6 + g, rows), do, TN)
-        ds = e * (dr - inner).astype(bf16)
-        dq = dot(both(q_buf, m, 3 + g, rows), ds, NN)
-        dk = dot(both(q_buf, m, g, rows), ds, NT)
-        dvv = dot(do, e, NT)
+    def heads_backward(m):
         co, si = rope[m, 0], rope[m, 1]
-        for part, t in ((0, dq * 0.125), (1, dk)):
-            t1, t2 = t[:32], t[32:]
-            t = jnp.concatenate([t1 * co + t2 * si, t2 * co - t1 * si], axis=0).astype(bf16)
-            p_buf[m, (3 * part + g) * 2, rows, :] = t[:, 0:256]
-            p_buf[m, (3 * part + g) * 2 + 1, rows, :] = t[:, 256:512]
-        dvv = dvv.astype(bf16)
-        p_buf[m, (6 + g) * 2, rows, :] = dvv[:, 0:256]
-        p_buf[m, (6 + g) * 2 + 1, rows, :] = dvv[:, 256:512]
-
-    def heads_backward(m, g):
-        for hh in range(4):
-            head_backward(m, g, hh)
+        pending = {}
+        for t in range(HEADS + 1):
+            if t < HEADS:
+                g, rows = t // 4, slice(64 * (t % 4), 64 * (t % 4) + 64)
+                do = (both(p_buf, m, 9 + g, rows).astype(f32) * inv[m, t, 0:1, :]).astype(bf16)
+                o = both(q_buf, m, 9 + g, rows)
+                inner = jnp.sum(do.astype(f32) * o.astype(f32), axis=0, keepdims=True)
+                pending[t] = (do, inner, dot(both(q_buf, m, 6 + g, rows), do, TN))
+            h = t - 1
+            if 0 <= h:
+                g, rows = h // 4, slice(64 * (h % 4), 64 * (h % 4) + 64)
+                do, inner, dr = pending.pop(h)
+                e = jnp.concatenate([e_buf[m, h * 2], e_buf[m, h * 2 + 1]], axis=1)
+                ds = e * (dr - inner).astype(bf16)
+                dvv = dot(do, e, NT)
+                dq = dot(both(q_buf, m, 3 + g, rows), ds, NN)
+                dk = dot(both(q_buf, m, g, rows), ds, NT)
+                for part, x in ((0, dq * 0.125), (1, dk)):
+                    t1, t2 = x[:32], x[32:]
+                    x = jnp.concatenate([t1 * co + t2 * si, t2 * co - t1 * si], axis=0).astype(bf16)
+                    p_buf[m, (3 * part + g) * 2, rows, :] = x[:, 0:256]
+                    p_buf[m, (3 * part + g) * 2 + 1, rows, :] = x[:, 256:512]
+                dvv = dvv.astype(bf16)
+                p_buf[m, (6 + g) * 2, rows, :] = dvv[:, 0:256]
+                p_buf[m, (6 + g) * 2 + 1, rows, :] = dvv[:, 256:512]
 
     def close_back(m, c):
         rows = rows_of(c)
         dp_t = jnp.concatenate([p_buf[m, fb * 2 + c] for fb in range(9)], axis=0)
         da = dot(dp_t, wi[:, 0 : 3 * D], TT) + xh[m, rows, :]
         finish_backward(m, c, da.astype(bf16))
+
+    def add(m, held, new):
+        return jnp.where(m == 0, new, held.astype(f32) + new).astype(bf16)
 
     def attention_weights(m):
         a_t = a_buf[m].T
@@ -415,32 +414,36 @@
                 [jnp.concatenate([p_buf[m, (3 * n + j) * 2], p_buf[m, (3 * n + j) * 2 + 1]], axis=1) for j in range(3)],
                 axis=0,
             )
-            dw[:, cols] = (dw[:, cols].astype(f32) + dot(a_t, d, NT)).astype(bf16)
+            dw[:, cols] = add(m, dw[:, cols], dot(a_t, d, NT))
             db[:, cols] += dot(jnp.ones((8, BLK), bf16), d, NT)
             return 0
 
         lax.fori_loop(0, 3, part, 0)
         o = jnp.concatenate([attended(m, 0), attended(m, 1)], axis=1)
-        dw[:, 3 * D :] = (dw[:, 3 * D :].astype(f32) + dot(o, y_buf[m], NN)).astype(bf16)
+        dw[:, 3 * D :] = add(m, dw[:, 3 * D :], dot(o, y_buf[m], NN))
 
     def feed_rows(m, c):
         arrive(m, c)
         rows = rows_of(c)
         a = a_buf[m, rows, :]
-        u = None
-        for n in range(4):
-            cols = slice(D * n, D * (n + 1))
-            h = dot(a, wi[:, cols], NN) + vec_in[:, cols]
-            h2 = h * h
-            s = 0.5 * jnp.tanh(h * (K0 + K1 * h2)) + 0.5
-            g = h * s
-            slope = (s + g * (1.0 - s) * (2.0 * K0 + 6.0 * K1 * h2)).astype(bf16)
-            g = g.astype(bf16)
-            for j in range(3):
-                q_buf[m, c * 12 + 3 * n + j] = g[:, 256 * j : 256 * (j + 1)]
-                e_buf[m, 3 * n + j, rows, :] = slope[:, 256 * j : 256 * (j + 1)]
-            t = dot(g, wd[cols, :], NN)
-            u = t if u is None else u + t
+        u, hidden = None, {}
+        for t in range(8):
+            if t < 6:
+                cols = slice(512 * t, 512 * (t + 1))
+                hidden[t] = dot(a, wi[:, cols], NN) + vec_in[:, cols]
+            n = t - 2
+            if n >= 0:
+                h = hidden.pop(n)
+                h2 = h * h
+                s = 0.5 * jnp.tanh(h * (K0 + K1 * h2)) + 0.5
+                g = h * s
+                slope = (s + g * (1.0 - s) * (2.0 * K0 + 6.0 * K1 * h2)).astype(bf16)
+                g = g.astype(bf16)
+                for j in range(2):
+                    q_buf[m, c * 12 + 2 * n + j] = g[:, 256 * j : 256 * (j + 1)]
+                    e_buf[m, 2 * n + j, rows, :] = slope[:, 256 * j : 256 * (j + 1)]
+                x = dot(g, wd[512 * n : 512 * (n + 1), :], NN)
+                u = x if u is None else u + x
         finish_forward(m, c, u + vec_out[:, 2 * D :] + a.astype(f32))
 
     def feed_forward(m):
@@ -451,19 +454,24 @@
 
         lax.fori_loop(0, 2, lambda c, _: (feed_rows(m, c), 0)[1], 0)
 
+    def feed_open_back(m, c):
+        arrive_back(m, c)
+        start_backward(m, c)
+
     def feed_rows_back(m, c):
-        arrive_back(m, c)
-        rows = rows_of(c)
-        dz, du = start_backward(m, c)
-        da = dz
-        for n in range(4):
-            cols = slice(D * n, D * (n + 1))
-            dg = dot(du, wd[cols, :], NT)
-            slope = jnp.concatenate([e_buf[m, 3 * n + j, rows, :] for j in range(3)], axis=1)
-            dh = (dg * slope.astype(f32)).astype(bf16)
-            for j in range(3):
-                p_buf[m, c * 12 + 3 * n + j] = dh[:, 256 * j : 256 * (j + 1)]
-            da = da + dot(dh, wi[:, cols], NT)
+        rows = rows_of(c)
+        du = y_buf[m, rows, :]
+        da, grads = xh[m, rows, :], {}
+        for t in range(5):
+            if t < 4:
+                grads[t] = dot(du, wd[D * t : D * (t + 1), :], NT)
+            n = t - 1
+            if n >= 0:
+                slope = jnp.concatenate([e_buf[m, 3 * n + j, rows, :] for j in range(3)], axis=1)
+                dh = (grads.pop(n) * slope.astype(f32)).astype(bf16)
+                for j in range(3):
+                    p_buf[m, c * 12 + 3 * n + j] = dh[:, 256 * j : 256 * (j + 1)]
+                da = da + dot(dh, wi[:, D * n : D * (n + 1)], NT)
         finish_backward(m, c, da.astype(bf16))
 
     def tile(buf, m, n):
@@ -474,7 +482,7 @@
     def feed_weights_down(m):
         def part(n, _):
             rows = pl.ds(pl.multiple_of(n * D, D), D)
-            dv[rows, :] = (dv[rows, :].astype(f32) + dot(tile(q_buf, m, n), y_buf[m], TN)).astype(bf16)
+            dv[rows, :] = add(m, dv[rows, :], dot(tile(q_buf, m, n), y_buf[m], TN))
             return 0
 
         lax.fori_loop(0, 4, part, 0)
@@ -483,54 +491,77 @@
         def part(n, _):
             cols = pl.ds(pl.multiple_of(n * D, D), D)
             dh = tile(p_buf, m, n)
-            dw[:, cols] = (dw[:, cols].astype(f32) + dot(a_buf[m], dh, TN)).astype(bf16)
+            dw[:, cols] = add(m, dw[:, cols], dot(a_buf[m], dh, TN))
             db[:, cols] += jnp.broadcast_to(jnp.sum(dh.astype(f32), axis=0, keepdims=True), (8, D))
             return 0
 
         lax.fori_loop(0, 4, part, 0)
 
-    def part_copy(grad, land, size, number, first, width, order, step, k, j):
-        slot = FIRST_SLOT[step] + k
-        return pltpu.make_async_remote_copy(
-            src_ref=grad.at[pl.ds(pl.multiple_of(j * size, size), size), pl.ds(first, width)],
-            dst_ref=land.at[pl.ds(slot * size, size), pl.ds(first, width)],
-            send_sem=rs_send.at[number, slot],
-            recv_sem=rs_recv.at[number, slot],
-            device_id={"dp": peer(order[step])},
-            device_id_type=MESH,
-        )
-
-    def step_copies(grad, land, size, number, part, step):
-        first, width, order = part
-        return [
-            part_copy(grad, land, size, number, first, width, order, step, k, j)
-            for k, j in enumerate(chunks(me, order, step, True))
-        ]
-
-    def send_step(*args):
-        for copy in step_copies(*args):
+    def landing(part, number, slot):
+        down, first, width, _ = part
+        if not down:
+            return wi.at[pl.ds(96 * slot, 96), pl.ds(first, width)]
+        piece = (number // 2) * 7 + slot
+        return e_buf.at[piece // 12, 12 + piece % 12, pl.ds(0, 384), pl.ds(128 * (number % 2), 128)]
+
+    def own_rows(part, j):
+        size = 384 if part[0] else 96
+        return pl.ds(pl.multiple_of(j * size, size), size), pl.ds(part[1], part[2])
+
+    def step_copies(number, step):
+        part = PARTS[number]
+        grad = dv if part[0] else dw
+        copies = []
+        for k, j in enumerate(chunks(me, part[3], step, True)):
+            slot = FIRST_SLOT[step] + k
+            copies.append(
+                pltpu.make_async_remote_copy(
+                    src_ref=grad.at[own_rows(part, j)],
+                    dst_ref=landing(part, number, slot),
+                    send_sem=rs_send.at[number, slot],
+                    recv_sem=rs_recv.at[number, slot],
+                    device_id={"dp": peer(part[3][step])},
+                    device_id_type=MESH,
+                )
+            )
+        return copies
+
+    def send_step(number, step):
+        for copy in step_copies(number, step):
             copy.start()
 
-    def take_step(grad, land, size, number, part, step):
-        first, width, order = part
-        cols = pl.ds(first, width)
-        copies = step_copies(grad, land, size, number, part, step)
-        for k, j in enumerate(chunks(me, order, step, False)):
+    def take_step(number, step):
+        part = PARTS[number]
+        grad = dv if part[0] else dw
+        copies = step_copies(number, step)
+        for k, j in enumerate(chunks(me, part[3], step, False)):
             copies[k].wait_recv()
-            slot = FIRST_SLOT[step] + k
-            rows = pl.ds(pl.multiple_of(j * size, size), size)
-            total = grad[rows, cols].astype(f32) + land[slot * size : (slot + 1) * size, cols].astype(f32)
+            index = own_rows(part, j)
+            total = grad[index].astype(f32) + landing(part, number, FIRST_SLOT[step] + k)[...].astype(f32)
             if step < 2:
-                grad[rows, cols] = total.astype(bf16)
-        return total
-
-    def wait_sends(grad, land, size, number, part):
-        for step in range(3):
-            for copy in step_copies(grad, land, size, number, part, step):
-                copy.wait_send()
-
-    down_parts = [(dv, wd, 384, i, part) for i, part in enumerate(PARTS_DOWN)]
-    in_parts = [(dw, wi, 96, len(PARTS_DOWN) + i, part) for i, part in enumerate(PARTS_IN)]
+                grad[index] = total.astype(bf16)
+        down, first, width, _ = part
+        if step < 2:
+            send_step(number, step + 1)
+        elif down:
+            xh[1, 0:384, first : first + width] = total
+        else:
+            q, off = first // D, first % D
+            xh[0, 96 * q : 96 * (q + 1), off : off + width] = total
+
+    def exchange(numbers, ahead, lag, started):
+        n = len(numbers)
+        for t in range(started, n + ahead + 2 * lag):
+            for step in (2, 1, 0):
+                i = t - ahead - lag * step
+                if 0 <= i < n:
+                    take_step(numbers[i], step)
+            if t < n:
+                send_step(numbers[t], 0)
+        for number in numbers:
+            for step in range(3):
+                for copy in step_copies(number, step):
+                    copy.wait_send()
 
     def weights_free():
         for b in range(3):
@@ -540,35 +571,51 @@
         for b in range(3):
             pl.semaphore_wait(free_sem.at[b], 1)
 
+    late = sec >= 2
+
+    def span(m):
+        return jnp.where(late, 0, m), jnp.where(late & (m == 0), 0, m + 1)
+
     def attention_backward(m):
         lax.fori_loop(0, 2, lambda c, _: (open_back(m, c), 0)[1], 0)
-        lax.fori_loop(0, 3, lambda g, _: (heads_backward(m, g), 0)[1], 0)
+        heads_backward(m)
         lax.fori_loop(0, 2, lambda c, _: (close_back(m, c), 0)[1], 0)
 
         @pl.when(m == MICRO - 1)
         def _():
             weights_free()
 
-        attention_weights(m)
+        lax.fori_loop(*span(m), lambda i, _: (attention_weights(i), 0)[1], 0)
 
     def feed_backward(m):
+        early = (sec == 1) & (m == MICRO - 1)
+        begin, end = span(m)
+
+        def down_products(begin, end):
+            lax.fori_loop(begin, end, lambda i, _: (feed_weights_down(i), 0)[1], 0)
+
+            @pl.when((begin < end) & (m == MICRO - 1))
+            def _():
+                for number in DOWN:
+                    send_step(number, 0)
+
+        lax.fori_loop(0, 2, lambda c, _: (feed_open_back(m, c), 0)[1], 0)
+        down_products(begin, jnp.where(early, end, begin))
         lax.fori_loop(0, 2, lambda c, _: (feed_rows_back(m, c), 0)[1], 0)
 
         @pl.when(m == MICRO - 1)
         def _():
             weights_free()
 
-        begin = jnp.where(sec == 3, 0, m)
-        end = jnp.where((sec == 3) & (m == 0), 0, m + 1)
-        lax.fori_loop(begin, end, lambda i, _: (feed_weights_down(i), 0)[1], 0)
-
-        @pl.when(m == MICRO - 1)
-        def _():
-            await_free()
-            for p in down_parts:
-                send_step(*p, 0)
-
+        down_products(begin, jnp.where(early, begin, end))
         lax.fori_loop(begin, end, lambda i, _: (feed_weights_in(i), 0)[1], 0)
+
+    @pl.when(even)
+    def _():
+        attention_tables(0)
+        for i in range(3):
+            b = jnp.broadcast_to(vec_in[:, D * i : D * (i + 1)], (128, D))
+            bias_t[D * i : D * (i + 1), :] = b.T
 
     pl.semaphore_wait(barrier, 3 + GROUP - 1)
 
@@ -596,12 +643,7 @@
 
     lax.fori_loop(0, 2 * MICRO, task, 0)
 
-    @pl.when(even)
-    def _():
-        await_free()
-
-    for p in in_parts:
-        send_step(*p, 0)
+    await_free()
 
     vec_send[...] = jnp.zeros_like(vec_send)
     outer = jnp.concatenate([acc[0:1, :], acc[1:2, :], acc[2:3, :]], axis=1)
@@ -623,35 +665,22 @@
     for k in range(1, GROUP):
         vec_copy(k).start()
 
-    for step in range(3):
-
-        @pl.when(odd)
-        def _():
-            for p in down_parts:
-                total = take_step(*p, step)
-                if step < 2:
-                    send_step(*p, step + 1)
-                else:
-                    first, width, _ = p[4]
-                    xh[1, 0:384, first : first + width] = total
-
-        for p in in_parts:
-            total = take_step(*p, step)
-            if step < 2:
-                send_step(*p, step + 1)
-            else:
-                first, width, _ = p[4]
-                for i in range(width // D):
-                    xh[0, 96 * (first // D + i) : 96 * (first // D + i + 1), :] = total[:, D * i : D * (i + 1)]
+    @pl.when(odd)
+    def _():
+        exchange(DOWN + IN, 6, 6, len(DOWN))
+
+    @pl.when(even)
+    def _():
+        exchange(IN, 4, 4, 0)
 
     @pl.when(even)
     def _():
         xh[1, 0:384, :] = jnp.zeros((384, D), f32)
 
-    outs = [pltpu.make_async_copy(xh.at[1, pl.ds(0, 384)], out_down, out_sem.at[4])]
+    outs = [pltpu.make_async_copy(xh.at[1, pl.ds(0, 384)], out_down.at[0], out_sem.at[4])]
     for i in range(4):
         outs.append(
-            pltpu.make_async_copy(xh.at[0, pl.ds(96 * i, 96)], out_in.at[:, pl.ds(D * i, D)], out_sem.at[i])
+            pltpu.make_async_copy(xh.at[0, pl.ds(96 * i, 96)], out_in.at[0, :, pl.ds(D * i, D)], out_sem.at[i])
         )
     for copy in outs:
         copy.start()
@@ -659,17 +688,11 @@
     for k in range(1, GROUP):
         vec_copy(k).wait_recv()
         total = total + vec_recv[k]
-    out_vec[...] = total
+    out_vec_in[...] = total[0:1, :]
+    out_vec_out[...] = total[1:2, 0:288]
 
     for k in range(1, GROUP):
         vec_copy(k).wait_send()
-    for p in in_parts:
-        wait_sends(*p)
-
-    @pl.when(odd)
-    def _():
-        for p in down_parts:
-            wait_sends(*p)
 
     for m in range(MICRO):
         for c in range(2):
@@ -705,18 +728,19 @@
     hbm = pl.BlockSpec(memory_space=pl.ANY)
     vmem = pl.BlockSpec(memory_space=pltpu.VMEM)
     V, S = pltpu.VMEM, pltpu.SemaphoreType.DMA
-    parts = len(PARTS_IN) + len(PARTS_DOWN)
-    mixed, in_grad, grad_in, grad_down, grad_vec = pl.pallas_call(
+    parts = len(PARTS)
+    mixed, in_grad, grad_in, grad_down, vec_a, vec_b = pl.pallas_call(
         functools.partial(kernel, low),
         out_shape=(
-            jax.ShapeDtypeStruct((MICRO, BLK, D // 4), bf16),
-            jax.ShapeDtypeStruct((MICRO, BLK, D // 4), bf16),
-            jax.ShapeDtypeStruct((D // GROUP, FF), f32),
-            jax.ShapeDtypeStruct((FF // GROUP, D), f32),
-            jax.ShapeDtypeStruct((8, 384), f32),
+            jax.ShapeDtypeStruct((MICRO, D // 4, BLK), bf16),
+            jax.ShapeDtypeStruct((MICRO, D // 4, BLK), bf16),
+            jax.ShapeDtypeStruct((1, D // GROUP, FF), f32),
+            jax.ShapeDtypeStruct((1, FF // GROUP, D), f32),
+            jax.ShapeDtypeStruct((1, FF // GROUP), f32),
+            jax.ShapeDtypeStruct((1, 3 * D // GROUP), f32),
         ),
         in_specs=[hbm, vmem, hbm, hbm, vmem, vmem, hbm],
-        out_specs=(hbm, hbm, hbm, hbm, vmem),
+        out_specs=(hbm, hbm, hbm, hbm, vmem, vmem),
         scratch_shapes=[
             V((D, FF), bf16),
             V((FF, D), bf16),
@@ -734,7 +758,7 @@
             V((3 * D, 128), f32),
             V((D, FF), bf16),
             V((FF, D), bf16),
-            V((4, MICRO, BLK, D // 4), bf16),
+            V((4, MICRO, D // 4, BLK), bf16),
             V((8, D), f32),
             V((8, FF), f32),
             V((GROUP, 8, 384), f32),
@@ -758,18 +782,18 @@
         compiler_params=pltpu.CompilerParams(
             collective_id=0, has_side_effects=True, vmem_limit_bytes=63 * MIB
         ),
-    )(inputs, segment_ids[:, None, :], w_in, w_down, vec_in, vec_out, cotangent)
-    vec_a, vec_b = grad_vec[0], grad_vec[1, :288]
+    )(inputs, segment_ids, w_in, w_down, vec_in, vec_out, cotangent)
     if low > 1:
         groups = [[g * low + i for i in range(low)] for g in range(GROUP)]
 
         def rest(value):
             return lax.psum_scatter(
-                value, "dp", scatter_dimension=0, axis_index_groups=groups, tiled=True
+                value, "dp", scatter_dimension=1, axis_index_groups=groups, tiled=True
             )
 
         grad_in, grad_down, vec_a, vec_b = rest(grad_in), rest(grad_down), rest(vec_a), rest(vec_b)
-    return mixed, in_grad, grad_in[None], grad_down[None], vec_a[None], vec_b[None]
+    mixed, in_grad = jnp.swapaxes(mixed, 1, 2), jnp.swapaxes(in_grad, 1, 2)
+    return mixed, in_grad, grad_in, grad_down, vec_a, vec_b
 
 
 def solution(mesh):

time: 227 us -> 181 us (0.80)
  Pallas kernels: 216 us -> 173 us
  local copies, waits for them, and re-layouts: 10 us -> 6.89 us
    pallas_call x1, Pallas kernels: 216 us -> 173 us  [on_device(): pl.pallas_call(functools.partial(kernel, low), out_shape=(jax.ShapeDtypeS...]
    slice x2 -> x0, local copies, waits for them, and re-layouts: 2.54 us -> none  [on_device(): vec_a, vec_b = (grad_vec[0], grad_vec[1, :288])]
    unnamed x8 -> x14, local copies, waits for them, and re-layouts: 6.19 us -> 6.89 us
where the time goes in v2:
time: 181 us
  Pallas kernels  173 us (96%)
  local copies, waits for them, and re-layouts  6.89 us (4%)
    pallas_call x1, Pallas kernels, on_device(): pl.pallas_call(functools.partial(kernel, low), out_shape=(jax.ShapeDtypeS...  173 us
    unnamed x14, local copies, waits for them, and re-layouts  6.89 us

profile of v2, /device:TPU:1, one launch (start us, length us, event | category | flops | bytes accessed | tf_op | source)
XLA Modules:
  0.0 180.9 jit_solution(13809575984228125837)
XLA Ops:
  0.6 173.3 %shard_map.118 = (bf16[2,192,512]{2,1,0:T(8,128)(2,1)}, bf16[2,192,512]{2,1,0:T(8,128)(2,1)}, f32[1,96,3072]{2,1,0:T(8,128)}, f32[1,384,768]{2,1,0:T(8,128)}, f32[1,384]{1,0:T(1,128)}, /*index=5*/f32[1,288]{1,0:T(1,128)}) custom-call(bf16[2,512,768]{2,1,0:T(8,128)(2,1)} %inputs.1, s32[2,512]{1,0:T(2,128)} %seg.1, bf16[1,768,3072]{2,1,0:T(8,128)(2,1)} %w_in.1, ...), custom_call_target="tpu_custom_call" | custom-call | tf_op jit(solution)/shard_map/pallas_call | solution.py:732
  174.0 0.0 copy-start.1
  174.0 1.9 %copy.19 = bf16[2,512,192]{1,2,0:T(8,128)(2,1)} copy(bf16[2,512,192]{1,2,0:T(8,128)(2,1)} %bitcast.3) | data formatting | bytes 786432
  175.8 0.0 copy-start
  175.8 1.9 %copy.20 = bf16[2,512,192]{1,2,0:T(8,128)(2,1)} copy(bf16[2,512,192]{1,2,0:T(8,128)(2,1)} %bitcast.2) | data formatting | bytes 786432
  177.7 0.0 copy-done.1
  177.7 1.0 copy.21
  178.7 0.0 copy-done
  178.7 0.0 copy-start.3
  178.7 0.0 copy-start.2
  178.7 1.0 copy.22
  179.7 0.0 copy-done.3
  179.7 0.6 copy.23
  180.3 0.0 copy-done.2
  180.3 0.6 copy.24
Async XLA Ops:
  174.0 3.7 %copy-start.1 = (f32[1,96,3072]{2,1,0:T(8,128)S(1)}, f32[1,96,3072]{2,1,0:T(8,128)}, u32[]{:S(2)}) copy-start(f32[1,96,3072]{2,1,0:T(8,128)} %get-tuple-element.26) | copy-start | bytes 3538948
  175.8 2.9 %copy-start = (f32[1,384,768]{2,1,0:T(8,128)S(1)}, f32[1,384,768]{2,1,0:T(8,128)}, u32[]{:S(2)}) copy-start(f32[1,384,768]{2,1,0:T(8,128)} %get-tuple-element.27) | copy-start | bytes 3538948
  178.7 1.0 copy-start.3
  178.7 1.6 copy-start.2

commit v3 on v2

--- a/solution.py
+++ b/solution.py
@@ -55,6 +55,8 @@
 PARTS = DOWN_PARTS + IN_PARTS
 DOWN = list(range(len(DOWN_PARTS)))
 IN = list(range(len(DOWN_PARTS), len(PARTS)))
+MOVED = 3
+AWAY = list(range(len(PARTS), len(PARTS) + MOVED))
 
 
 def kernel(
@@ -108,6 +110,12 @@
     rs_send,
     rs_recv,
     out_sem,
+    back,
+    move_send,
+    move_recv,
+    back_send,
+    back_recv,
+    room_sem,
 ):
     sec = lax.axis_index("section")
     dp = lax.axis_index("dp")
@@ -497,27 +505,33 @@
 
         lax.fori_loop(0, 4, part, 0)
 
-    def landing(part, number, slot):
-        down, first, width, _ = part
-        if not down:
-            return wi.at[pl.ds(96 * slot, 96), pl.ds(first, width)]
+    def part_of(number):
+        if number in AWAY:
+            return DOWN_PARTS[number - len(PARTS)], wd
+        return PARTS[number], dv if PARTS[number][0] else dw
+
+    def landing(number, slot):
+        part, grad = part_of(number)
+        if not part[0]:
+            return wi.at[pl.ds(96 * slot, 96), pl.ds(part[1], part[2])]
+        first = 0 if number in AWAY else 12
+        number = number % len(PARTS)
         piece = (number // 2) * 7 + slot
-        return e_buf.at[piece // 12, 12 + piece % 12, pl.ds(0, 384), pl.ds(128 * (number % 2), 128)]
+        return e_buf.at[piece // 12, first + piece % 12, pl.ds(0, 384), pl.ds(128 * (number % 2), 128)]
 
     def own_rows(part, j):
         size = 384 if part[0] else 96
         return pl.ds(pl.multiple_of(j * size, size), size), pl.ds(part[1], part[2])
 
     def step_copies(number, step):
-        part = PARTS[number]
-        grad = dv if part[0] else dw
+        part, grad = part_of(number)
         copies = []
         for k, j in enumerate(chunks(me, part[3], step, True)):
             slot = FIRST_SLOT[step] + k
             copies.append(
                 pltpu.make_async_remote_copy(
                     src_ref=grad.at[own_rows(part, j)],
-                    dst_ref=landing(part, number, slot),
+                    dst_ref=landing(number, slot),
                     send_sem=rs_send.at[number, slot],
                     recv_sem=rs_recv.at[number, slot],
                     device_id={"dp": peer(part[3][step])},
@@ -526,23 +540,54 @@
             )
         return copies
 
+    def move_copies(p):
+        copies = []
+        for j in range(GROUP):
+            index = own_rows(DOWN_PARTS[p], j)
+            copies.append(
+                pltpu.make_async_remote_copy(
+                    src_ref=dv.at[index],
+                    dst_ref=wd.at[index],
+                    send_sem=move_send.at[p, j],
+                    recv_sem=move_recv.at[p, j],
+                    device_id={"section": sec + 2},
+                    device_id_type=MESH,
+                )
+            )
+        return copies
+
+    def back_copy(p):
+        return pltpu.make_async_remote_copy(
+            src_ref=back.at[p],
+            dst_ref=back.at[p],
+            send_sem=back_send.at[p],
+            recv_sem=back_recv.at[p],
+            device_id={"section": sec - 2},
+            device_id_type=MESH,
+        )
+
     def send_step(number, step):
+        if step == 0 and number in AWAY:
+            for copy in move_copies(number - len(PARTS)):
+                copy.wait_recv()
         for copy in step_copies(number, step):
             copy.start()
 
     def take_step(number, step):
-        part = PARTS[number]
-        grad = dv if part[0] else dw
+        part, grad = part_of(number)
         copies = step_copies(number, step)
         for k, j in enumerate(chunks(me, part[3], step, False)):
             copies[k].wait_recv()
             index = own_rows(part, j)
-            total = grad[index].astype(f32) + landing(part, number, FIRST_SLOT[step] + k)[...].astype(f32)
+            total = grad[index].astype(f32) + landing(number, FIRST_SLOT[step] + k)[...].astype(f32)
             if step < 2:
                 grad[index] = total.astype(bf16)
         down, first, width, _ = part
         if step < 2:
             send_step(number, step + 1)
+        elif number in AWAY:
+            back[number - len(PARTS)] = total
+            back_copy(number - len(PARTS)).start()
         elif down:
             xh[1, 0:384, first : first + width] = total
         else:
@@ -594,20 +639,41 @@
         def down_products(begin, end):
             lax.fori_loop(begin, end, lambda i, _: (feed_weights_down(i), 0)[1], 0)
 
-            @pl.when((begin < end) & (m == MICRO - 1))
+        def rows(c, _):
+            feed_open_back(m, c)
+
+            @pl.when(early & (c == 1))
             def _():
-                for number in DOWN:
+                down_products(begin, end)
+                for number in DOWN[MOVED:]:
                     send_step(number, 0)
-
-        lax.fori_loop(0, 2, lambda c, _: (feed_open_back(m, c), 0)[1], 0)
-        down_products(begin, jnp.where(early, end, begin))
-        lax.fori_loop(0, 2, lambda c, _: (feed_rows_back(m, c), 0)[1], 0)
+                pl.semaphore_wait(room_sem, 1)
+                for p in range(MOVED):
+                    for copy in move_copies(p):
+                        copy.start()
+
+            feed_rows_back(m, c)
+            return 0
+
+        lax.fori_loop(0, 2, rows, 0)
 
         @pl.when(m == MICRO - 1)
         def _():
             weights_free()
 
-        down_products(begin, jnp.where(early, begin, end))
+        @pl.when((sec == 3) & (m == MICRO - 1))
+        def _():
+            pl.semaphore_signal(room_sem, inc=1, device_id={"section": 1}, device_id_type=MESH)
+
+        @pl.when(jnp.logical_not(early))
+        def _():
+            down_products(begin, end)
+
+        @pl.when((sec == 3) & (m == MICRO - 1))
+        def _():
+            for number in DOWN:
+                send_step(number, 0)
+
         lax.fori_loop(begin, end, lambda i, _: (feed_weights_in(i), 0)[1], 0)
 
     @pl.when(even)
@@ -665,9 +731,21 @@
     for k in range(1, GROUP):
         vec_copy(k).start()
 
-    @pl.when(odd)
+    @pl.when(sec == 1)
     def _():
-        exchange(DOWN + IN, 6, 6, len(DOWN))
+        exchange(DOWN[MOVED:] + IN, 6, 6, len(DOWN) - MOVED)
+        for p in range(MOVED):
+            back_copy(p).wait_recv()
+            first, width = DOWN_PARTS[p][1], DOWN_PARTS[p][2]
+            xh[1, 0:384, first : first + width] = back[p]
+            for copy in move_copies(p):
+                copy.wait_send()
+
+    @pl.when(sec == 3)
+    def _():
+        exchange(DOWN + IN + AWAY, 6, 6, len(DOWN))
+        for p in range(MOVED):
+            back_copy(p).wait_send()
 
     @pl.when(even)
     def _():
@@ -722,23 +800,34 @@
         copy.wait()
 
 
+def settle(*refs):
+    count = len(refs) // 2
+    sems = refs[-1]
+    copies = [pltpu.make_async_copy(refs[i], refs[count + i], sems.at[i]) for i in range(count)]
+    for copy in copies:
+        copy.start()
+    for copy in copies:
+        copy.wait()
+
+
 def on_device(inputs, segment_ids, w_in, w_down, vec_in, vec_out, cotangent):
     world = lax.axis_size("dp")
     low = world // GROUP
     hbm = pl.BlockSpec(memory_space=pl.ANY)
     vmem = pl.BlockSpec(memory_space=pltpu.VMEM)
     V, S = pltpu.VMEM, pltpu.SemaphoreType.DMA
-    parts = len(PARTS)
-    mixed, in_grad, grad_in, grad_down, vec_a, vec_b = pl.pallas_call(
+    parts = len(PARTS) + MOVED
+    shapes = (
+        jax.ShapeDtypeStruct((MICRO, D // 4, BLK), bf16),
+        jax.ShapeDtypeStruct((MICRO, D // 4, BLK), bf16),
+        jax.ShapeDtypeStruct((1, D // GROUP, FF), f32),
+        jax.ShapeDtypeStruct((1, FF // GROUP, D), f32),
+        jax.ShapeDtypeStruct((1, FF // GROUP), f32),
+        jax.ShapeDtypeStruct((1, 3 * D // GROUP), f32),
+    )
+    results = pl.pallas_call(
         functools.partial(kernel, low),
-        out_shape=(
-            jax.ShapeDtypeStruct((MICRO, D // 4, BLK), bf16),
-            jax.ShapeDtypeStruct((MICRO, D // 4, BLK), bf16),
-            jax.ShapeDtypeStruct((1, D // GROUP, FF), f32),
-            jax.ShapeDtypeStruct((1, FF // GROUP, D), f32),
-            jax.ShapeDtypeStruct((1, FF // GROUP), f32),
-            jax.ShapeDtypeStruct((1, 3 * D // GROUP), f32),
-        ),
+        out_shape=shapes,
         in_specs=[hbm, vmem, hbm, hbm, vmem, vmem, hbm],
         out_specs=(hbm, hbm, hbm, hbm, vmem, vmem),
         scratch_shapes=[
@@ -778,11 +867,24 @@
             S((parts, 7)),
             S((parts, 7)),
             S((5,)),
+            V((MOVED, FF // GROUP, 128), f32),
+            S((MOVED, GROUP)),
+            S((MOVED, GROUP)),
+            S((MOVED,)),
+            S((MOVED,)),
+            pltpu.SemaphoreType.REGULAR,
         ],
         compiler_params=pltpu.CompilerParams(
             collective_id=0, has_side_effects=True, vmem_limit_bytes=63 * MIB
         ),
     )(inputs, segment_ids, w_in, w_down, vec_in, vec_out, cotangent)
+    mixed, in_grad, grad_in, grad_down, vec_a, vec_b = pl.pallas_call(
+        settle,
+        out_shape=shapes,
+        in_specs=[vmem] * len(shapes),
+        out_specs=(hbm,) * len(shapes),
+        scratch_shapes=[S((len(shapes),))],
+    )(*results)
     if low > 1:
         groups = [[g * low + i for i in range(low)] for g in range(GROUP)]
 

time: 181 us -> 175 us (0.967)
  local copies, waits for them, and re-layouts: 6.89 us -> 0 us
    unnamed x14 -> x0, local copies, waits for them, and re-layouts: 6.89 us -> none
    pallas_call x1 -> x2, Pallas kernels: 173 us -> 174 us  [the longest x1 170 us: on_device(): pl.pallas_call(functools.partial(kernel, low), out_shape=shapes, in_specs...]
where the time goes in v3:
time: 175 us
  Pallas kernels  174 us (99%)
    pallas_call x1, Pallas kernels, on_device(): pl.pallas_call(functools.partial(kernel, low), out_shape=shapes, in_specs...  170 us
    pallas_call x1, Pallas kernels, on_device(): pl.pallas_call(settle, out_shape=shapes, in_specs=[vmem] * len(shapes), o...  3.59 us

profile of v3, /device:TPU:1, one launch (start us, length us, event | category | flops | bytes accessed | tf_op | source)
XLA Modules:
  0.0 174.6 jit_solution(8296395494480697173)
XLA Ops:
  0.6 170.2 %shard_map.118 = (bf16[2,192,512]{2,1,0:T(8,128)(2,1)}, bf16[2,192,512]{2,1,0:T(8,128)(2,1)}, f32[1,96,3072]{2,1,0:T(8,128)}, f32[1,384,768]{2,1,0:T(8,128)}, f32[1,384]{1,0:T(1,128)}, /*index=5*/f32[1,288]{1,0:T(1,128)}) custom-call(bf16[2,512,768]{2,1,0:T(8,128)(2,1)} %inputs.1, s32[2,512]{1,0:T(2,128)} %seg.1, bf16[1,768,3072]{2,1,0:T(8,128)(2,1)} %w_in.1, ...), custom_call_target="tpu_custom_call" | custom-call | tf_op jit(solution)/shard_map/pallas_call | solution.py:828
  170.8 3.6 %shard_map.119 = (bf16[2,192,512]{2,1,0:T(8,128)(2,1)}, bf16[2,192,512]{2,1,0:T(8,128)(2,1)}, f32[1,96,3072]{2,1,0:T(8,128)}, f32[1,384,768]{2,1,0:T(8,128)}, f32[1,384]{1,0:T(1,128)}, /*index=5*/f32[1,288]{1,0:T(1,128)}) custom-call(bf16[2,192,512]{2,1,0:T(8,128)(2,1)} %get-tuple-element.18.refs_0_, bf16[2,192,512]{2,1,0:T(8,128)(2,1)} %get-tuple-element.19.refs_1_, ...), custom_call_target="tpu_custom_call" | custom-call | tf_op jit(solution)/shard_map/pallas_call | solution.py:881

commit v4 on v3

--- a/solution.py
+++ b/solution.py
@@ -20,6 +20,8 @@
 NEG = -1e30
 K0 = math.sqrt(2.0 / math.pi)
 K1 = K0 * 0.044715
+LN2 = math.log(2.0)
+Q_SCALE = HEAD_DIM**-0.5 / LN2
 MIB = 1 << 20
 bf16, f32 = jnp.bfloat16, jnp.float32
 MESH = pl.DeviceIdType.MESH
@@ -40,23 +42,12 @@
     return (value // (1 << b)) % 2
 
 
-def chunks(me, order, step, flip):
-    base = sum(bit(me, order[i]) * (1 << order[i]) for i in range(step))
-    own = bit(me, order[step])
-    base = base + ((1 - own) if flip else own) * (1 << order[step])
-    free = order[step + 1 :]
-    out = []
-    for k in range(1 << len(free)):
-        out.append(base + sum(((k >> i) & 1) << free[i] for i in range(len(free))))
-    return out
-
-
-FIRST_SLOT = (0, 4, 6)
 PARTS = DOWN_PARTS + IN_PARTS
 DOWN = list(range(len(DOWN_PARTS)))
 IN = list(range(len(DOWN_PARTS), len(PARTS)))
 MOVED = 3
 AWAY = list(range(len(PARTS), len(PARTS) + MOVED))
+ORDER_3 = DOWN + IN[:5] + AWAY[:1] + IN[5:7] + AWAY[1:2] + IN[7:9] + AWAY[2:] + IN[9:]
 
 
 def kernel(
@@ -126,8 +117,8 @@
     def peer(b):
         return dp + (1 - 2 * bit(me, b)) * (1 << b) * low
 
-    load_wi = pltpu.make_async_copy(w_in.at[0], wi, w_sem.at[0])
-    load_wd = pltpu.make_async_copy(w_down.at[0], wd, w_sem.at[1])
+    load_wi = pltpu.make_async_copy(w_in, wi, w_sem.at[0])
+    load_wd = pltpu.make_async_copy(w_down, wd, w_sem.at[1])
 
     def load_a(m):
         return pltpu.make_async_copy(inputs.at[m], a_buf.at[m], load_sem.at[m])
@@ -159,6 +150,18 @@
 
     acc[...] = jnp.zeros_like(acc)
     db[...] = jnp.zeros_like(db)
+
+    def w_cols(first, last):
+        return wi[:, :, :, :, first:last].reshape(D, last - first)
+
+    def w_rows(first, last):
+        pieces = []
+        while first < last:
+            j, start = first // 384, first % 384
+            stop = min(384, start + last - first)
+            pieces.append(wd[j // 4, j // 2 % 2, j % 2, start:stop, :])
+            first += stop - start
+        return jnp.concatenate(pieces, axis=0)
 
     def rows_of(c):
         return pl.ds(pl.multiple_of(c * CH, CH), CH)
@@ -304,7 +307,7 @@
         a = a_buf[m, rows, :]
         co, si = rope[m, 0, :, rows], rope[m, 1, :, rows]
         for part in range(3):
-            p = dot(wi[:, D * part : D * (part + 1)], a, TT)
+            p = dot(w_cols(D * part, D * (part + 1)), a, TT)
             b = bias_t[D * part : D * (part + 1), :]
             p = p + jnp.concatenate([b, b], axis=1)
             if part < 2:
@@ -313,7 +316,7 @@
                 r1 = t1 * co[None] - t2 * si[None]
                 r2 = t2 * co[None] + t1 * si[None]
                 if part == 0:
-                    r1, r2 = r1 * 0.125, r2 * 0.125
+                    r1, r2 = r1 * Q_SCALE, r2 * Q_SCALE
                 p = jnp.concatenate([r1[:, None], r2[:, None]], axis=1).reshape(D, CH)
             p = p.astype(bf16)
             for j in range(3):
@@ -332,11 +335,11 @@
             if 0 <= h < HEADS:
                 st = scores.pop(h)
                 peak = jnp.max(st, axis=0, keepdims=True)
-                e = jnp.exp(st - peak)
+                e = jnp.exp2(st - peak)
                 r = 1.0 / jnp.sum(e, axis=0, keepdims=True)
                 e = e.astype(bf16)
-                e_buf[m, h * 2] = e[:, 0:256]
-                e_buf[m, h * 2 + 1] = e[:, 256:512]
+                e_buf[m, h // 6, h % 6 * 2] = e[:, 0:256]
+                e_buf[m, h // 6, h % 6 * 2 + 1] = e[:, 256:512]
                 inv[m, h] = jnp.broadcast_to(r, (8, BLK))
                 weights[h] = (e, r)
             h = t - 2
@@ -352,7 +355,7 @@
 
     def close(m, c):
         rows = rows_of(c)
-        u = dot(attended(m, c), wi[:, 3 * D :], TN) + vec_out[:, 2 * D :]
+        u = dot(attended(m, c), w_cols(3 * D, FF), TN) + vec_out[:, 2 * D :]
         finish_forward(m, c, u + a_buf[m, rows, :].astype(f32))
 
     def attention_forward(m):
@@ -372,7 +375,7 @@
         arrive_back(m, c)
         rows = rows_of(c)
         du = start_backward(m, c)
-        do = dot(wi[:, 3 * D :], du, NT).astype(bf16)
+        do = dot(w_cols(3 * D, FF), du, NT).astype(bf16)
         for j in range(3):
             p_buf[m, (9 + j) * 2 + c] = do[256 * j : 256 * (j + 1), :]
 
@@ -390,12 +393,12 @@
             if 0 <= h:
                 g, rows = h // 4, slice(64 * (h % 4), 64 * (h % 4) + 64)
                 do, inner, dr = pending.pop(h)
-                e = jnp.concatenate([e_buf[m, h * 2], e_buf[m, h * 2 + 1]], axis=1)
+                e = jnp.concatenate([e_buf[m, h // 6, h % 6 * 2], e_buf[m, h // 6, h % 6 * 2 + 1]], axis=1)
                 ds = e * (dr - inner).astype(bf16)
                 dvv = dot(do, e, NT)
                 dq = dot(both(q_buf, m, 3 + g, rows), ds, NN)
                 dk = dot(both(q_buf, m, g, rows), ds, NT)
-                for part, x in ((0, dq * 0.125), (1, dk)):
+                for part, x in ((0, dq * 0.125), (1, dk * LN2)):
                     t1, t2 = x[:32], x[32:]
                     x = jnp.concatenate([t1 * co + t2 * si, t2 * co - t1 * si], axis=0).astype(bf16)
                     p_buf[m, (3 * part + g) * 2, rows, :] = x[:, 0:256]
@@ -407,11 +410,13 @@
     def close_back(m, c):
         rows = rows_of(c)
         dp_t = jnp.concatenate([p_buf[m, fb * 2 + c] for fb in range(9)], axis=0)
-        da = dot(dp_t, wi[:, 0 : 3 * D], TT) + xh[m, rows, :]
+        da = dot(dp_t, w_cols(0, 3 * D), TT) + xh[m, rows, :]
         finish_backward(m, c, da.astype(bf16))
 
-    def add(m, held, new):
-        return jnp.where(m == 0, new, held.astype(f32) + new).astype(bf16)
+    def add(m, ref, index, new):
+        held = ref[index]
+        new = new.reshape(held.shape)
+        ref[index] = jnp.where(m == 0, new, held.astype(f32) + new).astype(bf16)
 
     def attention_weights(m):
         a_t = a_buf[m].T
@@ -422,13 +427,13 @@
                 [jnp.concatenate([p_buf[m, (3 * n + j) * 2], p_buf[m, (3 * n + j) * 2 + 1]], axis=1) for j in range(3)],
                 axis=0,
             )
-            dw[:, cols] = add(m, dw[:, cols], dot(a_t, d, NT))
+            add(m, dw, (slice(None),) * 4 + (cols,), dot(a_t, d, NT))
             db[:, cols] += dot(jnp.ones((8, BLK), bf16), d, NT)
             return 0
 
         lax.fori_loop(0, 3, part, 0)
         o = jnp.concatenate([attended(m, 0), attended(m, 1)], axis=1)
-        dw[:, 3 * D :] = add(m, dw[:, 3 * D :], dot(o, y_buf[m], NN))
+        add(m, dw, (slice(None),) * 4 + (slice(3 * D, FF),), dot(o, y_buf[m], NN))
 
     def feed_rows(m, c):
         arrive(m, c)
@@ -438,7 +443,7 @@
         for t in range(8):
             if t < 6:
                 cols = slice(512 * t, 512 * (t + 1))
-                hidden[t] = dot(a, wi[:, cols], NN) + vec_in[:, cols]
+                hidden[t] = dot(a, w_cols(512 * t, 512 * (t + 1)), NN) + vec_in[:, cols]
             n = t - 2
             if n >= 0:
                 h = hidden.pop(n)
@@ -449,8 +454,8 @@
                 g = g.astype(bf16)
                 for j in range(2):
                     q_buf[m, c * 12 + 2 * n + j] = g[:, 256 * j : 256 * (j + 1)]
-                    e_buf[m, 2 * n + j, rows, :] = slope[:, 256 * j : 256 * (j + 1)]
-                x = dot(g, wd[512 * n : 512 * (n + 1), :], NN)
+                    e_buf[m, 0, 2 * n + j, rows, :] = slope[:, 256 * j : 256 * (j + 1)]
+                x = dot(g, w_rows(512 * n, 512 * (n + 1)), NN)
                 u = x if u is None else u + x
         finish_forward(m, c, u + vec_out[:, 2 * D :] + a.astype(f32))
 
@@ -472,14 +477,14 @@
         da, grads = xh[m, rows, :], {}
         for t in range(5):
             if t < 4:
-                grads[t] = dot(du, wd[D * t : D * (t + 1), :], NT)
+                grads[t] = dot(du, w_rows(D * t, D * (t + 1)), NT)
             n = t - 1
             if n >= 0:
-                slope = jnp.concatenate([e_buf[m, 3 * n + j, rows, :] for j in range(3)], axis=1)
+                slope = jnp.concatenate([e_buf[m, 0, 3 * n + j, rows, :] for j in range(3)], axis=1)
                 dh = (grads.pop(n) * slope.astype(f32)).astype(bf16)
                 for j in range(3):
                     p_buf[m, c * 12 + 3 * n + j] = dh[:, 256 * j : 256 * (j + 1)]
-                da = da + dot(dh, wi[:, D * n : D * (n + 1)], NT)
+                da = da + dot(dh, w_cols(D * n, D * (n + 1)), NT)
         finish_backward(m, c, da.astype(bf16))
 
     def tile(buf, m, n):
@@ -489,8 +494,7 @@
 
     def feed_weights_down(m):
         def part(n, _):
-            rows = pl.ds(pl.multiple_of(n * D, D), D)
-            dv[rows, :] = add(m, dv[rows, :], dot(tile(q_buf, m, n), y_buf[m], TN))
+            add(m, dv, (n // 2, n % 2), dot(tile(q_buf, m, n), y_buf[m], TN))
             return 0
 
         lax.fori_loop(0, 4, part, 0)
@@ -499,7 +503,7 @@
         def part(n, _):
             cols = pl.ds(pl.multiple_of(n * D, D), D)
             dh = tile(p_buf, m, n)
-            dw[:, cols] = add(m, dw[:, cols], dot(a_buf[m], dh, TN))
+            add(m, dw, (slice(None),) * 4 + (cols,), dot(a_buf[m], dh, TN))
             db[:, cols] += jnp.broadcast_to(jnp.sum(dh.astype(f32), axis=0, keepdims=True), (8, D))
             return 0
 
@@ -510,51 +514,47 @@
             return DOWN_PARTS[number - len(PARTS)], wd
         return PARTS[number], dv if PARTS[number][0] else dw
 
-    def landing(number, slot):
+    def landing(number, step):
+        part = part_of(number)[0]
+        if not part[0]:
+            place = ((0,), (1, 0), (1, 1, 0))[step]
+            rest = (slice(None),) * (4 - len(place))
+            return wi.at[place + rest + (pl.ds(part[1], part[2]),)]
+        half = 0 if number in AWAY else 1
+        number = number % len(PARTS)
+        q, corner = number // 2, (pl.ds(0, 384), pl.ds(128 * (number % 2), 128))
+        place = ((slice(None), half, pl.ds(2 * q, 2)), (0, half, pl.ds(6 + 2 * q, 2)), (1, half, 6 + q))[step]
+        return e_buf.at[place + corner]
+
+    def share_of(number, step, flip):
         part, grad = part_of(number)
-        if not part[0]:
-            return wi.at[pl.ds(96 * slot, 96), pl.ds(part[1], part[2])]
-        first = 0 if number in AWAY else 12
-        number = number % len(PARTS)
-        piece = (number // 2) * 7 + slot
-        return e_buf.at[piece // 12, first + piece % 12, pl.ds(0, 384), pl.ds(128 * (number % 2), 128)]
-
-    def own_rows(part, j):
-        size = 384 if part[0] else 96
-        return pl.ds(pl.multiple_of(j * size, size), size), pl.ds(part[1], part[2])
-
-    def step_copies(number, step):
-        part, grad = part_of(number)
-        copies = []
-        for k, j in enumerate(chunks(me, part[3], step, True)):
-            slot = FIRST_SLOT[step] + k
-            copies.append(
-                pltpu.make_async_remote_copy(
-                    src_ref=grad.at[own_rows(part, j)],
-                    dst_ref=landing(number, slot),
-                    send_sem=rs_send.at[number, slot],
-                    recv_sem=rs_recv.at[number, slot],
-                    device_id={"dp": peer(part[3][step])},
-                    device_id_type=MESH,
-                )
-            )
-        return copies
-
-    def move_copies(p):
-        copies = []
-        for j in range(GROUP):
-            index = own_rows(DOWN_PARTS[p], j)
-            copies.append(
-                pltpu.make_async_remote_copy(
-                    src_ref=dv.at[index],
-                    dst_ref=wd.at[index],
-                    send_sem=move_send.at[p, j],
-                    recv_sem=move_recv.at[p, j],
-                    device_id={"section": sec + 2},
-                    device_id_type=MESH,
-                )
-            )
-        return copies
+        order = part[3]
+        index = [slice(None)] * 3
+        for i in range(step + 1):
+            own = bit(me, order[i])
+            index[2 - order[i]] = 1 - own if flip and i == step else own
+        return grad.at[tuple(index) + (slice(None), pl.ds(part[1], part[2]))]
+
+    def step_copy(number, step):
+        return pltpu.make_async_remote_copy(
+            src_ref=share_of(number, step, True),
+            dst_ref=landing(number, step),
+            send_sem=rs_send.at[number, step],
+            recv_sem=rs_recv.at[number, step],
+            device_id={"dp": peer(part_of(number)[0][3][step])},
+            device_id_type=MESH,
+        )
+
+    def move_copy(p):
+        index = (slice(None),) * 4 + (pl.ds(DOWN_PARTS[p][1], DOWN_PARTS[p][2]),)
+        return pltpu.make_async_remote_copy(
+            src_ref=dv.at[index],
+            dst_ref=wd.at[index],
+            send_sem=move_send.at[p],
+            recv_sem=move_recv.at[p],
+            device_id={"section": sec + 2},
+            device_id_type=MESH,
+        )
 
     def back_copy(p):
         return pltpu.make_async_remote_copy(
@@ -566,33 +566,37 @@
             device_id_type=MESH,
         )
 
+    def result_copy(number):
+        down, first, width, _ = PARTS[number]
+        cols = pl.ds(first, width)
+        if down:
+            return pltpu.make_async_copy(xh.at[1, pl.ds(0, 384), cols], out_down.at[0, :, cols], out_sem.at[number])
+        rows = pl.ds(96 * (first // D), 96)
+        return pltpu.make_async_copy(xh.at[0, rows, pl.ds(first % D, width)], out_in.at[0, :, cols], out_sem.at[number])
+
     def send_step(number, step):
         if step == 0 and number in AWAY:
-            for copy in move_copies(number - len(PARTS)):
-                copy.wait_recv()
-        for copy in step_copies(number, step):
-            copy.start()
+            move_copy(number - len(PARTS)).wait_recv()
+        step_copy(number, step).start()
 
     def take_step(number, step):
-        part, grad = part_of(number)
-        copies = step_copies(number, step)
-        for k, j in enumerate(chunks(me, part[3], step, False)):
-            copies[k].wait_recv()
-            index = own_rows(part, j)
-            total = grad[index].astype(f32) + landing(number, FIRST_SLOT[step] + k)[...].astype(f32)
-            if step < 2:
-                grad[index] = total.astype(bf16)
-        down, first, width, _ = part
+        step_copy(number, step).wait_recv()
+        down, first, width, _ = part_of(number)[0]
+        share = share_of(number, step, False)
+        total = share[...].astype(f32) + landing(number, step)[...].astype(f32)
         if step < 2:
+            share[...] = total.astype(bf16)
             send_step(number, step + 1)
         elif number in AWAY:
             back[number - len(PARTS)] = total
             back_copy(number - len(PARTS)).start()
         elif down:
             xh[1, 0:384, first : first + width] = total
+            result_copy(number).start()
         else:
             q, off = first // D, first % D
             xh[0, 96 * q : 96 * (q + 1), off : off + width] = total
+            result_copy(number).start()
 
     def exchange(numbers, ahead, lag, started):
         n = len(numbers)
@@ -605,8 +609,7 @@
                 send_step(numbers[t], 0)
         for number in numbers:
             for step in range(3):
-                for copy in step_copies(number, step):
-                    copy.wait_send()
+                step_copy(number, step).wait_send()
 
     def weights_free():
         for b in range(3):
@@ -649,8 +652,7 @@
                     send_step(number, 0)
                 pl.semaphore_wait(room_sem, 1)
                 for p in range(MOVED):
-                    for copy in move_copies(p):
-                        copy.start()
+                    move_copy(p).start()
 
             feed_rows_back(m, c)
             return 0
@@ -731,6 +733,13 @@
     for k in range(1, GROUP):
         vec_copy(k).start()
 
+    zeros = pltpu.make_async_copy(xh.at[1, pl.ds(0, 384)], out_down.at[0], out_sem.at[0])
+
+    @pl.when(even)
+    def _():
+        xh[1, 0:384, :] = jnp.zeros((384, D), f32)
+        zeros.start()
+
     @pl.when(sec == 1)
     def _():
         exchange(DOWN[MOVED:] + IN, 6, 6, len(DOWN) - MOVED)
@@ -738,12 +747,12 @@
             back_copy(p).wait_recv()
             first, width = DOWN_PARTS[p][1], DOWN_PARTS[p][2]
             xh[1, 0:384, first : first + width] = back[p]
-            for copy in move_copies(p):
-                copy.wait_send()
+            result_copy(p).start()
+            move_copy(p).wait_send()
 
     @pl.when(sec == 3)
     def _():
-        exchange(DOWN + IN + AWAY, 6, 6, len(DOWN))
+        exchange(ORDER_3, 6, 6, len(DOWN))
         for p in range(MOVED):
             back_copy(p).wait_send()
 
@@ -751,17 +760,6 @@
     def _():
         exchange(IN, 4, 4, 0)
 
-    @pl.when(even)
-    def _():
-        xh[1, 0:384, :] = jnp.zeros((384, D), f32)
-
-    outs = [pltpu.make_async_copy(xh.at[1, pl.ds(0, 384)], out_down.at[0], out_sem.at[4])]
-    for i in range(4):
-        outs.append(
-            pltpu.make_async_copy(xh.at[0, pl.ds(96 * i, 96)], out_in.at[0, :, pl.ds(D * i, D)], out_sem.at[i])
-        )
-    for copy in outs:
-        copy.start()
     total = vec_send[me]
     for k in range(1, GROUP):
         vec_copy(k).wait_recv()
@@ -796,18 +794,43 @@
                 for k in range(3):
                     share_copy(m, c, k, mixed, mix_recv).wait_send()
 
-    for copy in outs:
-        copy.wait()
+    for number in IN:
+        result_copy(number).wait()
+
+    @pl.when(odd)
+    def _():
+        for number in DOWN:
+            result_copy(number).wait()
+
+    @pl.when(even)
+    def _():
+        zeros.wait()
 
 
 def settle(*refs):
-    count = len(refs) // 2
-    sems = refs[-1]
-    copies = [pltpu.make_async_copy(refs[i], refs[count + i], sems.at[i]) for i in range(count)]
-    for copy in copies:
-        copy.start()
-    for copy in copies:
-        copy.wait()
+    count = (len(refs) - 2) // 3
+    given, taken, held = refs[:count], refs[count : 2 * count], refs[2 * count : 3 * count]
+    sem_in, sem_out = refs[-2:]
+    steps = []
+    for i in range(count):
+        rows = given[i].shape[1]
+        cut = rows // 2 if len(given[i].shape) == 3 else rows
+        for k in range(rows // cut):
+            index = (slice(None), pl.ds(k * cut, cut))
+            n = len(steps)
+            steps.append(
+                (
+                    pltpu.make_async_copy(given[i].at[index], held[i].at[index], sem_in.at[n]),
+                    pltpu.make_async_copy(held[i].at[index], taken[i].at[index], sem_out.at[n]),
+                )
+            )
+    for first, _ in steps:
+        first.start()
+    for first, second in steps:
+        first.wait()
+        second.start()
+    for _, second in steps:
+        second.wait()
 
 
 def on_device(inputs, segment_ids, w_in, w_down, vec_in, vec_out, cotangent):
@@ -831,12 +854,12 @@
         in_specs=[hbm, vmem, hbm, hbm, vmem, vmem, hbm],
         out_specs=(hbm, hbm, hbm, hbm, vmem, vmem),
         scratch_shapes=[
-            V((D, FF), bf16),
-            V((FF, D), bf16),
+            V((2, 2, 2, 96, FF), bf16),
+            V((2, 2, 2, 384, D), bf16),
             V((MICRO, BLK, D), bf16),
             V((MICRO, BLK, D), bf16),
             V((MICRO, BLK, D), bf16),
-            V((MICRO, 24, 512, 256), bf16),
+            V((MICRO, 2, 12, 512, 256), bf16),
             V((MICRO, 24, 256, 256), bf16),
             V((MICRO, 24, 256, 256), bf16),
             V((MICRO, BLK, D), f32),
@@ -845,8 +868,8 @@
             V((MICRO, 2, HEAD_DIM // 2, BLK), f32),
             V((MICRO, HEADS, 8, BLK), f32),
             V((3 * D, 128), f32),
-            V((D, FF), bf16),
-            V((FF, D), bf16),
+            V((2, 2, 2, 96, FF), bf16),
+            V((2, 2, 2, 384, D), bf16),
             V((4, MICRO, D // 4, BLK), bf16),
             V((8, D), f32),
             V((8, FF), f32),
@@ -864,12 +887,12 @@
             S((GROUP,)),
             S((GROUP,)),
             pltpu.SemaphoreType.REGULAR((3,)),
-            S((parts, 7)),
-            S((parts, 7)),
-            S((5,)),
+            S((parts, 3)),
+            S((parts, 3)),
+            S((len(PARTS),)),
             V((MOVED, FF // GROUP, 128), f32),
-            S((MOVED, GROUP)),
-            S((MOVED, GROUP)),
+            S((MOVED,)),
+            S((MOVED,)),
             S((MOVED,)),
             S((MOVED,)),
             pltpu.SemaphoreType.REGULAR,
@@ -877,13 +900,13 @@
         compiler_params=pltpu.CompilerParams(
             collective_id=0, has_side_effects=True, vmem_limit_bytes=63 * MIB
         ),
-    )(inputs, segment_ids, w_in, w_down, vec_in, vec_out, cotangent)
+    )(inputs, segment_ids, w_in.reshape(2, 2, 2, 96, FF), w_down.reshape(2, 2, 2, 384, D), vec_in, vec_out, cotangent)
     mixed, in_grad, grad_in, grad_down, vec_a, vec_b = pl.pallas_call(
         settle,
         out_shape=shapes,
-        in_specs=[vmem] * len(shapes),
+        in_specs=[hbm] * len(shapes),
         out_specs=(hbm,) * len(shapes),
-        scratch_shapes=[S((len(shapes),))],
+        scratch_shapes=[V(x.shape, x.dtype) for x in shapes] + [S((10,)), S((10,))],
     )(*results)
     if low > 1:
         groups = [[g * low + i for i in range(low)] for g in range(GROUP)]

time: 175 us -> 167 us (0.954)
  Pallas kernels: 174 us -> 166 us
    pallas_call x1, Pallas kernels: 170 us -> 162 us  [on_device(): pl.pallas_call(functools.partial(kernel, low), out_shape=shapes, in_specs...]
where the time goes in v4:
time: 167 us; the launch traced here: 166 us
  Pallas kernels  166 us (99%)
    pallas_call x1, Pallas kernels, on_device(): pl.pallas_call(functools.partial(kernel, low), out_shape=shapes, in_specs...  162 us

profile of v4, /device:TPU:1, one launch (start us, length us, event | category | flops | bytes accessed | tf_op | source)
XLA Modules:
  0.0 166.3 jit_solution(5831693391900924273)
XLA Ops:
  0.6 162.3 %shard_map.118 = (bf16[2,192,512]{2,1,0:T(8,128)(2,1)}, bf16[2,192,512]{2,1,0:T(8,128)(2,1)}, f32[1,96,3072]{2,1,0:T(8,128)}, f32[1,384,768]{2,1,0:T(8,128)}, f32[1,384]{1,0:T(1,128)}, /*index=5*/f32[1,288]{1,0:T(1,128)}) custom-call(bf16[2,512,768]{2,1,0:T(8,128)(2,1)} %inputs.1, s32[2,512]{1,0:T(2,128)} %seg.1, bf16[2,2,2,96,3072]{4,3,2,1,0:T(8,128)(2,1)} %bitcast.4, ...), custom_call_target="tpu_custom_call" | custom-call | tf_op jit(solution)/shard_map/pallas_call | solution.py:851
  162.9 3.2 %shard_map.119 = (bf16[2,192,512]{2,1,0:T(8,128)(2,1)}, bf16[2,192,512]{2,1,0:T(8,128)(2,1)}, f32[1,96,3072]{2,1,0:T(8,128)}, f32[1,384,768]{2,1,0:T(8,128)}, f32[1,384]{1,0:T(1,128)}, /*index=5*/f32[1,288]{1,0:T(1,128)}) custom-call(bf16[2,192,512]{2,1,0:T(8,128)(2,1)} %get-tuple-element.18.refs_0_, bf16[2,192,512]{2,1,0:T(8,128)(2,1)} %get-tuple-element.19.refs_1_, ...), custom_call_target="tpu_custom_call" | custom-call | tf_op jit(solution)/shard_map/pallas_call | solution.py:904

commit v5 on v4

--- a/solution.py
+++ b/solution.py
@@ -47,7 +47,7 @@
 IN = list(range(len(DOWN_PARTS), len(PARTS)))
 MOVED = 3
 AWAY = list(range(len(PARTS), len(PARTS) + MOVED))
-ORDER_3 = DOWN + IN[:5] + AWAY[:1] + IN[5:7] + AWAY[1:2] + IN[7:9] + AWAY[2:] + IN[9:]
+ORDER_3 = DOWN + IN[:4] + AWAY[:1] + IN[4:6] + AWAY[1:2] + IN[6:8] + AWAY[2:] + IN[8:]
 
 
 def kernel(
@@ -203,10 +203,12 @@
         cols = rows_of(c)
         return pltpu.make_async_copy(split.at[k, m, :, cols], out.at[m, :, cols], mix_send.at[k, m, c])
 
-    def share(m, c, value, own, out, recv):
+    def fill(m, c, value):
         flipped = value.T
         for k in range(4):
             split[k, m, :, rows_of(c)] = flipped[192 * k : 192 * (k + 1), :]
+
+    def share(m, c, own, out, recv):
         for k in range(4):
             if k == own:
                 own_copy(m, c, k, out).start()
@@ -253,7 +255,8 @@
 
         @pl.when(sec == 3)
         def _():
-            share(m, c, y, 3, mixed, mix_recv)
+            for k in range(4):
+                dw[m, c, 0, 0:64, D * k : D * (k + 1)] = y[64 * k : 64 * (k + 1), :]
 
     def start_backward(m, c):
         rows = rows_of(c)
@@ -286,7 +289,8 @@
 
         @pl.when(sec == 0)
         def _():
-            share(m, c, da, 0, in_grad, grad_recv)
+            fill(m, c, da)
+            share(m, c, 0, in_grad, grad_recv)
 
     def attention_tables(m):
         row = seg[pl.ds(m, 1), :].astype(f32)
@@ -598,7 +602,7 @@
             xh[0, 96 * q : 96 * (q + 1), off : off + width] = total
             result_copy(number).start()
 
-    def exchange(numbers, ahead, lag, started):
+    def exchange(numbers, ahead, lag, started, also=None):
         n = len(numbers)
         for t in range(started, n + ahead + 2 * lag):
             for step in (2, 1, 0):
@@ -607,6 +611,8 @@
                     take_step(numbers[i], step)
             if t < n:
                 send_step(numbers[t], 0)
+            if also is not None and t == started + 7:
+                also()
         for number in numbers:
             for step in range(3):
                 step_copy(number, step).wait_send()
@@ -675,6 +681,13 @@
         def _():
             for number in DOWN:
                 send_step(number, 0)
+
+            def give(i, _):
+                y = [dw[i // 2, i % 2, 0, 0:64, D * k : D * (k + 1)] for k in range(4)]
+                fill(i // 2, i % 2, jnp.concatenate(y, axis=0))
+                return 0
+
+            lax.fori_loop(0, 4, give, 0)
 
         lax.fori_loop(begin, end, lambda i, _: (feed_weights_in(i), 0)[1], 0)
 
@@ -752,13 +765,18 @@
 
     @pl.when(sec == 3)
     def _():
-        exchange(ORDER_3, 6, 6, len(DOWN))
+        def shares():
+            for m in range(MICRO):
+                for c in range(2):
+                    share(m, c, 3, mixed, mix_recv)
+
+        exchange(ORDER_3, 6, 6, len(DOWN), shares)
         for p in range(MOVED):
             back_copy(p).wait_send()
 
     @pl.when(even)
     def _():
-        exchange(IN, 4, 4, 0)
+        exchange(IN, 5, 5, 0)
 
     total = vec_send[me]
     for k in range(1, GROUP):

time: 167 us -> 166 us (level)
  no operation moved by 1% of the time
where the time goes in v5:
time: 166 us
  Pallas kernels  165 us (99%)
    pallas_call x1, Pallas kernels, on_device(): pl.pallas_call(functools.partial(kernel, low), out_shape=shapes, in_specs...  162 us

profile of v5, /device:TPU:1, one launch (start us, length us, event | category | flops | bytes accessed | tf_op | source)
XLA Modules:
  0.0 165.8 jit_solution(8532333197128577695)
XLA Ops:
  0.6 161.7 %shard_map.118 = (bf16[2,192,512]{2,1,0:T(8,128)(2,1)}, bf16[2,192,512]{2,1,0:T(8,128)(2,1)}, f32[1,96,3072]{2,1,0:T(8,128)}, f32[1,384,768]{2,1,0:T(8,128)}, f32[1,384]{1,0:T(1,128)}, /*index=5*/f32[1,288]{1,0:T(1,128)}) custom-call(bf16[2,512,768]{2,1,0:T(8,128)(2,1)} %inputs.1, s32[2,512]{1,0:T(2,128)} %seg.1, bf16[2,2,2,96,3072]{4,3,2,1,0:T(8,128)(2,1)} %bitcast.4, ...), custom_call_target="tpu_custom_call" | custom-call | tf_op jit(solution)/shard_map/pallas_call | solution.py:869
  162.4 3.2 %shard_map.119 = (bf16[2,192,512]{2,1,0:T(8,128)(2,1)}, bf16[2,192,512]{2,1,0:T(8,128)(2,1)}, f32[1,96,3072]{2,1,0:T(8,128)}, f32[1,384,768]{2,1,0:T(8,128)}, f32[1,384]{1,0:T(1,128)}, /*index=5*/f32[1,288]{1,0:T(1,128)}) custom-call(bf16[2,192,512]{2,1,0:T(8,128)(2,1)} %get-tuple-element.18.refs_0_, bf16[2,192,512]{2,1,0:T(8,128)(2,1)} %get-tuple-element.19.refs_1_, ...), custom_call_target="tpu_custom_call" | custom-call | tf_op jit(solution)/shard_map/pallas_call | solution.py:922

commit v6 on v5

--- a/solution.py
+++ b/solution.py
@@ -117,7 +117,11 @@
     def peer(b):
         return dp + (1 - 2 * bit(me, b)) * (1 << b) * low
 
-    load_wi = pltpu.make_async_copy(w_in, wi, w_sem.at[0])
+    def load_cols(first, last, n):
+        cols = (slice(None),) * 4 + (pl.ds(first, last - first),)
+        return pltpu.make_async_copy(w_in.at[cols], wi.at[cols], w_sem.at[n])
+
+    load_wi, load_wo = load_cols(0, 3 * D, 0), load_cols(3 * D, FF, 2)
     load_wd = pltpu.make_async_copy(w_down, wd, w_sem.at[1])
 
     def load_a(m):
@@ -132,6 +136,7 @@
             load_a(m).start()
 
     load_wi.start()
+    load_wo.start()
 
     @pl.when(odd)
     def _():
@@ -373,6 +378,11 @@
 
         lax.fori_loop(0, 2, lambda c, _: (project(m, c), 0)[1], 0)
         heads_forward(m)
+
+        @pl.when(m == 0)
+        def _():
+            load_wo.wait()
+
         lax.fori_loop(0, 2, lambda c, _: (close(m, c), 0)[1], 0)
 
     def open_back(m, c):
@@ -467,6 +477,7 @@
         @pl.when(m == 0)
         def _():
             load_wi.wait()
+            load_wo.wait()
             load_wd.wait()
 
         lax.fori_loop(0, 2, lambda c, _: (feed_rows(m, c), 0)[1], 0)
@@ -479,16 +490,16 @@
         rows = rows_of(c)
         du = y_buf[m, rows, :]
         da, grads = xh[m, rows, :], {}
-        for t in range(5):
-            if t < 4:
-                grads[t] = dot(du, w_rows(D * t, D * (t + 1)), NT)
-            n = t - 1
+        for t in range(8):
+            if t < 6:
+                grads[t] = dot(du, w_rows(512 * t, 512 * (t + 1)), NT)
+            n = t - 2
             if n >= 0:
-                slope = jnp.concatenate([e_buf[m, 0, 3 * n + j, rows, :] for j in range(3)], axis=1)
+                slope = jnp.concatenate([e_buf[m, 0, 2 * n + j, rows, :] for j in range(2)], axis=1)
                 dh = (grads.pop(n) * slope.astype(f32)).astype(bf16)
-                for j in range(3):
-                    p_buf[m, c * 12 + 3 * n + j] = dh[:, 256 * j : 256 * (j + 1)]
-                da = da + dot(dh, w_cols(D * n, D * (n + 1)), NT)
+                for j in range(2):
+                    p_buf[m, c * 12 + 2 * n + j] = dh[:, 256 * j : 256 * (j + 1)]
+                da = da + dot(dh, w_cols(512 * n, 512 * (n + 1)), NT)
         finish_backward(m, c, da.astype(bf16))
 
     def tile(buf, m, n):
@@ -893,7 +904,7 @@
             V((8, FF), f32),
             V((GROUP, 8, 384), f32),
             V((GROUP, 8, 384), f32),
-            S((2,)),
+            S((3,)),
             S((MICRO,)),
             S((MICRO, 2)),
             S((MICRO, 2)),

time: 166 us -> 166 us (level)
  no operation moved by 1% of the time
where the time goes in v6:
time: 166 us
  Pallas kernels  165 us (99%)
    pallas_call x1, Pallas kernels, on_device(): pl.pallas_call(functools.partial(kernel, low), out_shape=shapes, in_specs...  162 us

profile of v6, /device:TPU:1, one launch (start us, length us, event | category | flops | bytes accessed | tf_op | source)
XLA Modules:
  0.0 165.8 jit_solution(16643901007304833438)
XLA Ops:
  0.6 161.7 %shard_map.118 = (bf16[2,192,512]{2,1,0:T(8,128)(2,1)}, bf16[2,192,512]{2,1,0:T(8,128)(2,1)}, f32[1,96,3072]{2,1,0:T(8,128)}, f32[1,384,768]{2,1,0:T(8,128)}, f32[1,384]{1,0:T(1,128)}, /*index=5*/f32[1,288]{1,0:T(1,128)}) custom-call(bf16[2,512,768]{2,1,0:T(8,128)(2,1)} %inputs.1, s32[2,512]{1,0:T(2,128)} %seg.1, bf16[2,2,2,96,3072]{4,3,2,1,0:T(8,128)(2,1)} %bitcast.4, ...), custom_call_target="tpu_custom_call" | custom-call | tf_op jit(solution)/shard_map/pallas_call | solution.py:880
  162.4 3.2 %shard_map.119 = (bf16[2,192,512]{2,1,0:T(8,128)(2,1)}, bf16[2,192,512]{2,1,0:T(8,128)(2,1)}, f32[1,96,3072]{2,1,0:T(8,128)}, f32[1,384,768]{2,1,0:T(8,128)}, f32[1,384]{1,0:T(1,128)}, /*index=5*/f32[1,288]{1,0:T(1,128)}) custom-call(bf16[2,192,512]{2,1,0:T(8,128)(2,1)} %get-tuple-element.18.refs_0_, bf16[2,192,512]{2,1,0:T(8,128)(2,1)} %get-tuple-element.19.refs_1_, ...), custom_call_target="tpu_custom_call" | custom-call | tf_op jit(solution)/shard_map/pallas_call | solution.py:933
